TPU v7x, 512 devices: a whole 4x4x16 slice. The times are simulated.
512 devices in a mesh: pipe: 16 (over z), dp: 8 (over y, x_hi), tensor: 4 (over x_lo, core).
Axes of the slice: x: 4 (x_hi: 2, x_lo: 2; x = x_hi * 2 + x_lo), y: 4, z: 16, core: 2. Of those that a mesh axis runs over, the one named last changes fastest.
Arguments:
- inputs: bfloat16 [2, 8, 64, 7168], P(None, 'dp', None, 'tensor'), may hold values from -6 to 6
- lengths: int32 [2, 8, 4], P(None, 'dp'), may hold values from 1 to 32, 64 in all within a row
- w_down: bfloat16 [16, 7168, 512], P('pipe', 'tensor', 'dp'), may hold values from -0.0625 to 0.0625
- w_query: bfloat16 [16, 512, 512], P('pipe', 'dp', 'tensor'), may hold values from -0.25 to 0.25
- w_out: bfloat16 [16, 512, 7168], P('pipe', 'dp', 'tensor'), may hold values from -0.25 to 0.25
- gain_latent: bfloat16 [16, 512], P('pipe'), may hold values from 0.25 to 1.75
- readout: bfloat16 [7168], P('tensor'), may hold values from -0.0625 to 0.0625
Outputs:
- latents: bfloat16 [16, 2, 8, 64, 512], P('pipe', None, 'dp')
- scores: float32 [2, 8, 64], P(None, 'dp')
Inputs may be any that keep to these rules, and one draw needn't show every extreme that they name: Each micro-batch's lengths sum to 64; the longest is exactly 32.
All inputs are finite; a program needn't handle non-finite values.
Results may differ from a plain program's by a relative error of at most 0.035.
Values may be sent and summed in bfloat16 or wider, within the bound.
A program may use at most 64 MiB of HBM per device.

v0:
```python
import jax
import jax.numpy as jnp
from jax import lax
from jax.sharding import PartitionSpec as P


def from_partner(block, axis, stride):
    count = lax.axis_size(axis)
    route = []
    for low in range(count):
        high = low | 1 << stride
        if high != low and high < count:
            route += [(low, high), (high, low)]
    return lax.ppermute(block, axis, route)


def from_behind(block, axis, distance):
    devices = range(lax.axis_size(axis))
    route = [(i - distance, i) for i in devices if i - distance in devices]
    return lax.ppermute(block, axis, route)


def doc_mask(row_lengths, seq):
    ends = jnp.cumsum(row_lengths)
    positions = jnp.arange(seq)
    doc = jnp.sum((positions[:, None] >= ends[None, :]).astype(jnp.int32), axis=1)
    return (doc[:, None] == doc[None, :]) & (positions[None, :] <= positions[:, None])


def normalize(part, gain):
    scale = lax.rsqrt(jnp.mean(part * part, axis=1, keepdims=True) + 1e-06)
    return (part * scale * gain.astype(jnp.float32)).astype(jnp.bfloat16)


def run_layer(hidden, mask, down, query_map, out_map, gain, active):

    def compress():
        return jnp.dot(hidden, down, preferred_element_type=jnp.float32)

    def empty_part():
        return jnp.zeros((hidden.shape[0], down.shape[1]), jnp.float32)

    part = lax.cond(active, compress, empty_part)
    whole = lax.psum(part, "tensor")
    latent = normalize(whole, gain)
    query = jnp.dot(latent, query_map, preferred_element_type=jnp.float32).astype(jnp.bfloat16)
    width = query_map.shape[1]
    keys = lax.dynamic_slice_in_dim(latent, lax.axis_index("tensor") * width, width, 1)
    logits = lax.psum(jnp.dot(query, keys.T, preferred_element_type=jnp.float32), "tensor")
    logits = logits / jnp.sqrt(jnp.float32(latent.shape[1]))
    logits = jnp.where(mask, logits, jnp.float32(-1e30))
    weights = jax.nn.softmax(logits, axis=1).astype(jnp.bfloat16)
    mixed = jnp.dot(weights, latent, preferred_element_type=jnp.float32).astype(jnp.bfloat16)

    def project():
        return jnp.dot(mixed, out_map, preferred_element_type=jnp.float32)

    def empty_update():
        return jnp.zeros((hidden.shape[0], out_map.shape[1]), jnp.float32)

    update = lax.cond(active, project, empty_update)
    return ((hidden.astype(jnp.float32) + update).astype(jnp.bfloat16), latent)


def body(inputs, lengths, w_down, w_query, w_out, gain_latent, readout):
    sections = lax.axis_size("pipe")
    rank = lax.axis_index("pipe")
    micro = inputs.shape[1]
    seq = inputs.shape[2]
    mirror_down, mirror_query, mirror_out, mirror_gain = (w_down, w_query, w_out, gain_latent)
    for bit in range(sections.bit_length() - 1):
        mirror_down, mirror_query, mirror_out, mirror_gain = from_partner(
            (mirror_down, mirror_query, mirror_out, mirror_gain), "pipe", bit
        )
    own_down, own_query, own_out, far_down, far_query, far_out = (
        lax.all_gather(w_down, "dp", axis=2, tiled=True),
        lax.all_gather(w_query, "dp", axis=1, tiled=True),
        lax.all_gather(w_out, "dp", axis=1, tiled=True),
        lax.all_gather(mirror_down, "dp", axis=2, tiled=True),
        lax.all_gather(mirror_query, "dp", axis=1, tiled=True),
        lax.all_gather(mirror_out, "dp", axis=1, tiled=True),
    )
    own_weights = (own_down[0], own_query[0], own_out[0], gain_latent[0])
    far_weights = (far_down[0], far_query[0], far_out[0], mirror_gain[0])
    head = readout.astype(jnp.float32)

    def advance(tick_index, side, buffer, weights, position, first, last, kept, exits):
        slot = tick_index - position
        active = (slot >= 0) & (slot < micro)
        index = jnp.clip(slot, 0, micro - 1)
        entering = lax.dynamic_index_in_dim(inputs[side], index, 0, keepdims=False)
        entry = jnp.where(first, entering, buffer)
        mask = doc_mask(lax.dynamic_index_in_dim(lengths[side], index, 0, keepdims=False), seq)
        result, latent = run_layer(
            entry, mask, weights[0], weights[1], weights[2], weights[3], active
        )
        previous = kept[side, index]
        kept = kept.at[side, index].set(jnp.where(active, latent, previous))
        value = jnp.sum(result.astype(jnp.float32) * head[None, :], axis=1)
        exits = exits.at[side, index].add(jnp.where(active & last, value, jnp.zeros_like(value)))
        return (result, kept, exits)

    def tick(tick_index, carry):
        left_buffer, right_buffer, kept, exits = carry
        left_out, kept, exits = advance(
            tick_index,
            0,
            left_buffer,
            own_weights,
            rank,
            rank == 0,
            rank == sections - 1,
            kept,
            exits,
        )
        right_out, kept, exits = advance(
            tick_index,
            1,
            right_buffer,
            far_weights,
            sections - 1 - rank,
            rank == sections - 1,
            rank == 0,
            kept,
            exits,
        )
        left_buffer = from_behind(left_out, "pipe", 1)
        right_buffer = from_behind(right_out, "pipe", -1)
        return (left_buffer, right_buffer, kept, exits)

    latent_width = own_down.shape[2]
    width = inputs.shape[3]
    start = (
        jnp.zeros((seq, width), jnp.bfloat16),
        jnp.zeros((seq, width), jnp.bfloat16),
        jnp.zeros((2, micro, seq, latent_width), jnp.bfloat16),
        jnp.zeros((2, micro, seq), jnp.float32),
    )
    left_buffer, right_buffer, kept, exits = lax.fori_loop(0, sections + micro - 1, tick, start)
    scores = lax.psum(exits, ("pipe", "tensor"))
    return (kept[None], scores)


def solution(mesh):
    in_specs = (
        P(None, "dp", None, "tensor"),
        P(None, "dp", None),
        P("pipe", "tensor", "dp"),
        P("pipe", "dp", "tensor"),
        P("pipe", "dp", "tensor"),
        P("pipe", None),
        P("tensor"),
    )
    out_specs = (P("pipe", None, "dp", None, None), P(None, "dp", None))
    return jax.shard_map(body, mesh=mesh, in_specs=in_specs, out_specs=out_specs, check_vma=False)
```

profile of v0, /device:TPU:1, one launch (start us, length us, event | category | flops | bytes accessed | tf_op | source)
XLA Modules:
  0.0 1865.1 jit_solution(1107245311152016136)
XLA Ops:
  7.9 4.4 collective-permute-start.2
  15.9 6.7 collective-permute-start.3
  22.6 8.9 collective-permute-done.3
  31.5 9.9 collective-permute-start.4
  41.4 19.8 %collective-permute-done.4 = bf16[1,1792,64]{1,2,0:T(8,128)(2,1)S(1)} collective-permute-done((bf16[1,1792,64]{1,2,0:T(8,128)(2,1)S(1)}, bf16[1,1792,64]{1,2,0:T(8,128)(2,1)S(1)}, u32[]{:S(2)}, u32[]{:S(2)}) %collective-permute-start.4) | collective-permute-done | bytes 229408 | tf_op jit(solution)/shard_map/ppermute | solution.py:14
  61.2 17.9 collective-permute-start.5
  79.0 14.7 collective-permute-done.5
  97.1 6.8 collective-permute-done.14
  105.8 13.3 collective-permute-done.15
  122.2 21.7 %collective-permute-done.16 = bf16[1,64,1792]{2,1,0:T(8,128)(2,1)S(1)} collective-permute-done((bf16[1,64,1792]{2,1,0:T(8,128)(2,1)S(1)}, bf16[1,64,1792]{2,1,0:T(8,128)(2,1)S(1)}, u32[]{:S(2)}, u32[]{:S(2)}) %collective-permute-start.16) | collective-permute-done | bytes 229408 | tf_op jit(solution)/shard_map/ppermute | solution.py:14
  143.8 5.0 collective-permute-start.17
  148.8 20.4 %collective-permute-done.17 = bf16[1,64,1792]{2,1,0:T(8,128)(2,1)S(1)} collective-permute-done((bf16[1,64,1792]{2,1,0:T(8,128)(2,1)S(1)}, bf16[1,64,1792]{2,1,0:T(8,128)(2,1)S(1)}, u32[]{:S(2)}, u32[]{:S(2)}) %collective-permute-start.17) | collective-permute-done | bytes 229408 | tf_op jit(solution)/shard_map/ppermute | solution.py:14
  181.5 4.2 collective-permute-start.7
  189.0 6.6 collective-permute-start.8
  195.6 6.6 collective-permute-start.13
  202.2 33.6 %all_gather.19 = bf16[1,512,128]{2,1,0:T(8,128)(2,1)} all-gather(bf16[1,64,128]{2,1,0:T(8,128)(2,1)} %param.28), channel_id=1, replica_groups=mesh['pipe'=16,'dp'=8,'tensor'=4] {'dp'}, dimensions={1}, use_global_device_ids=true | all-gather | bytes 147456 | tf_op jit(solution)/shard_map/all_gather | solution.py:77
  235.8 5.0 collective-permute-start.9
  242.5 6.3 collective-permute-done.9
  248.9 30.3 %all_gather.22 = bf16[1,512,128]{2,1,0:T(8,128)(2,1)} all-gather(bf16[1,64,128]{2,1,0:T(8,128)(2,1)S(1)} %collective-permute-done.13), channel_id=1, replica_groups=mesh['pipe'=16,'dp'=8,'tensor'=4] {'dp'}, dimensions={1}, use_global_device_ids=true | all-gather | bytes 147456 | tf_op jit(solution)/shard_map/all_gather | solution.py:80
  282.0 3.8 copy.14
  285.9 9.4 all-gather.11.cloned.1.call-done
  296.0 1455.4 %while.25 = (s32[]{:T(128)}, bf16[64,1792]{1,0:T(8,128)(2,1)S(1)}, bf16[64,1792]{1,0:T(8,128)(2,1)S(1)}, bf16[2,1,64,512]{3,2,1,0:T(8,128)(2,1)}, f32[2,1,64]{2,...) while((s32[]{:T(128)}, bf16[64,1792]{1,0:T(8,128)(2,1)S(1)}, ...), condition=%wide.region_29.30_spmd, body=%wide.region_2.29_spmd.sunk | while | flops 499419744 | bytes 18871112 | solution.py:139
  300.9 53.4 %all-reduce.8.cloned.1.call-done = (f32[64,512]{1,0:T(8,128)}, f32[64,512]{1,0:T(8,128)}) async-done(((f32[64,512]{1,0:T(8,128)}, f32[64,512]{1,0:T(8,128)}), (f32[64,512]{1,0:T(8,128)}, f32[64,512]{1,0:T(8,128)})) %all-reduce.8.cloned.1.call-update) | async-done | bytes 262160 | tf_op jit(solution)/shard_map/while/body/eval_jaxpr/psum | solution.py:44
  363.2 10.7 all-reduce.5
  382.6 3.8 collective-permute-done.1
  390.9 54.0 %all-reduce.8.cloned.1.call-done = (f32[64,512]{1,0:T(8,128)}, f32[64,512]{1,0:T(8,128)}) async-done(((f32[64,512]{1,0:T(8,128)}, f32[64,512]{1,0:T(8,128)}), (f32[64,512]{1,0:T(8,128)}, f32[64,512]{1,0:T(8,128)})) %all-reduce.8.cloned.1.call-update) | async-done | bytes 262160 | tf_op jit(solution)/shard_map/while/body/eval_jaxpr/psum | solution.py:44
  453.7 10.7 all-reduce.5
  465.9 5.3 collective-permute-start
  484.1 51.6 %all-reduce.8.cloned.1.call-done = (f32[64,512]{1,0:T(8,128)}, f32[64,512]{1,0:T(8,128)}) async-done(((f32[64,512]{1,0:T(8,128)}, f32[64,512]{1,0:T(8,128)}), (f32[64,512]{1,0:T(8,128)}, f32[64,512]{1,0:T(8,128)})) %all-reduce.8.cloned.1.call-update) | async-done | bytes 262160 | tf_op jit(solution)/shard_map/while/body/eval_jaxpr/psum | solution.py:44
  544.5 10.7 all-reduce.5
  564.7 5.8 collective-permute-done.1
  575.0 51.5 %all-reduce.8.cloned.1.call-done = (f32[64,512]{1,0:T(8,128)}, f32[64,512]{1,0:T(8,128)}) async-done(((f32[64,512]{1,0:T(8,128)}, f32[64,512]{1,0:T(8,128)}), (f32[64,512]{1,0:T(8,128)}, f32[64,512]{1,0:T(8,128)})) %all-reduce.8.cloned.1.call-update) | async-done | bytes 262160 | tf_op jit(solution)/shard_map/while/body/eval_jaxpr/psum | solution.py:44
  635.2 10.7 all-reduce.5
  655.5 3.8 collective-permute-done.1
  663.7 53.5 %all-reduce.8.cloned.1.call-done = (f32[64,512]{1,0:T(8,128)}, f32[64,512]{1,0:T(8,128)}) async-done(((f32[64,512]{1,0:T(8,128)}, f32[64,512]{1,0:T(8,128)}), (f32[64,512]{1,0:T(8,128)}, f32[64,512]{1,0:T(8,128)})) %all-reduce.8.cloned.1.call-update) | async-done | bytes 262160 | tf_op jit(solution)/shard_map/while/body/eval_jaxpr/psum | solution.py:44
  726.0 10.7 all-reduce.5
  746.2 3.8 collective-permute-done.1
  754.5 53.2 %all-reduce.8.cloned.1.call-done = (f32[64,512]{1,0:T(8,128)}, f32[64,512]{1,0:T(8,128)}) async-done(((f32[64,512]{1,0:T(8,128)}, f32[64,512]{1,0:T(8,128)}), (f32[64,512]{1,0:T(8,128)}, f32[64,512]{1,0:T(8,128)})) %all-reduce.8.cloned.1.call-update) | async-done | bytes 262160 | tf_op jit(solution)/shard_map/while/body/eval_jaxpr/psum | solution.py:44
  816.5 10.7 all-reduce.5
  845.0 53.6 %all-reduce.8.cloned.1.call-done = (f32[64,512]{1,0:T(8,128)}, f32[64,512]{1,0:T(8,128)}) async-done(((f32[64,512]{1,0:T(8,128)}, f32[64,512]{1,0:T(8,128)}), (f32[64,512]{1,0:T(8,128)}, f32[64,512]{1,0:T(8,128)})) %all-reduce.8.cloned.1.call-update) | async-done | bytes 262160 | tf_op jit(solution)/shard_map/while/body/eval_jaxpr/psum | solution.py:44
  907.4 10.7 all-reduce.5
  935.8 54.4 %all-reduce.8.cloned.1.call-done = (f32[64,512]{1,0:T(8,128)}, f32[64,512]{1,0:T(8,128)}) async-done(((f32[64,512]{1,0:T(8,128)}, f32[64,512]{1,0:T(8,128)}), (f32[64,512]{1,0:T(8,128)}, f32[64,512]{1,0:T(8,128)})) %all-reduce.8.cloned.1.call-update) | async-done | bytes 262160 | tf_op jit(solution)/shard_map/while/body/eval_jaxpr/psum | solution.py:44
  999.0 10.7 all-reduce.5
  1027.5 55.5 %all-reduce.8.cloned.1.call-done = (f32[64,512]{1,0:T(8,128)}, f32[64,512]{1,0:T(8,128)}) async-done(((f32[64,512]{1,0:T(8,128)}, f32[64,512]{1,0:T(8,128)}), (f32[64,512]{1,0:T(8,128)}, f32[64,512]{1,0:T(8,128)})) %all-reduce.8.cloned.1.call-update) | async-done | bytes 262160 | tf_op jit(solution)/shard_map/while/body/eval_jaxpr/psum | solution.py:44
  1091.8 10.7 all-reduce.5
  1120.3 55.1 %all-reduce.8.cloned.1.call-done = (f32[64,512]{1,0:T(8,128)}, f32[64,512]{1,0:T(8,128)}) async-done(((f32[64,512]{1,0:T(8,128)}, f32[64,512]{1,0:T(8,128)}), (f32[64,512]{1,0:T(8,128)}, f32[64,512]{1,0:T(8,128)})) %all-reduce.8.cloned.1.call-update) | async-done | bytes 262160 | tf_op jit(solution)/shard_map/while/body/eval_jaxpr/psum | solution.py:44
  1184.2 10.7 all-reduce.5
  1204.4 3.8 collective-permute-done.1
  1212.7 54.0 %all-reduce.8.cloned.1.call-done = (f32[64,512]{1,0:T(8,128)}, f32[64,512]{1,0:T(8,128)}) async-done(((f32[64,512]{1,0:T(8,128)}, f32[64,512]{1,0:T(8,128)}), (f32[64,512]{1,0:T(8,128)}, f32[64,512]{1,0:T(8,128)})) %all-reduce.8.cloned.1.call-update) | async-done | bytes 262160 | tf_op jit(solution)/shard_map/while/body/eval_jaxpr/psum | solution.py:44
  1275.5 10.7 all-reduce.5
  1304.0 53.2 %all-reduce.8.cloned.1.call-done = (f32[64,512]{1,0:T(8,128)}, f32[64,512]{1,0:T(8,128)}) async-done(((f32[64,512]{1,0:T(8,128)}, f32[64,512]{1,0:T(8,128)}), (f32[64,512]{1,0:T(8,128)}, f32[64,512]{1,0:T(8,128)})) %all-reduce.8.cloned.1.call-update) | async-done | bytes 262160 | tf_op jit(solution)/shard_map/while/body/eval_jaxpr/psum | solution.py:44
  1366.0 10.7 all-reduce.5
  1394.4 53.2 %all-reduce.8.cloned.1.call-done = (f32[64,512]{1,0:T(8,128)}, f32[64,512]{1,0:T(8,128)}) async-done(((f32[64,512]{1,0:T(8,128)}, f32[64,512]{1,0:T(8,128)}), (f32[64,512]{1,0:T(8,128)}, f32[64,512]{1,0:T(8,128)})) %all-reduce.8.cloned.1.call-update) | async-done | bytes 262160 | tf_op jit(solution)/shard_map/while/body/eval_jaxpr/psum | solution.py:44
  1456.4 10.7 all-reduce.5
  1484.9 53.2 %all-reduce.8.cloned.1.call-done = (f32[64,512]{1,0:T(8,128)}, f32[64,512]{1,0:T(8,128)}) async-done(((f32[64,512]{1,0:T(8,128)}, f32[64,512]{1,0:T(8,128)}), (f32[64,512]{1,0:T(8,128)}, f32[64,512]{1,0:T(8,128)})) %all-reduce.8.cloned.1.call-update) | async-done | bytes 262160 | tf_op jit(solution)/shard_map/while/body/eval_jaxpr/psum | solution.py:44
  1546.9 10.7 all-reduce.5
  1567.1 5.8 collective-permute-done.1
  1577.4 51.5 %all-reduce.8.cloned.1.call-done = (f32[64,512]{1,0:T(8,128)}, f32[64,512]{1,0:T(8,128)}) async-done(((f32[64,512]{1,0:T(8,128)}, f32[64,512]{1,0:T(8,128)}), (f32[64,512]{1,0:T(8,128)}, f32[64,512]{1,0:T(8,128)})) %all-reduce.8.cloned.1.call-update) | async-done | bytes 262160 | tf_op jit(solution)/shard_map/while/body/eval_jaxpr/psum | solution.py:44
  1637.7 10.7 all-reduce.5
  1649.9 5.3 collective-permute-start
  1670.0 49.4 %all-reduce.8.cloned.1.call-done = (f32[64,512]{1,0:T(8,128)}, f32[64,512]{1,0:T(8,128)}) async-done(((f32[64,512]{1,0:T(8,128)}, f32[64,512]{1,0:T(8,128)}), (f32[64,512]{1,0:T(8,128)}, f32[64,512]{1,0:T(8,128)})) %all-reduce.8.cloned.1.call-update) | async-done | bytes 262160 | tf_op jit(solution)/shard_map/while/body/eval_jaxpr/psum | solution.py:44
  1728.2 10.7 all-reduce.5
  1747.5 3.8 collective-permute-done.1
  1751.4 106.9 %psum.59 = f32[2,1,64]{2,1,0:T(1,128)} all-reduce(f32[2,1,64]{2,1,0:T(1,128)S(1)} %get-tuple-element.553), channel_id=1, replica_groups=mesh['pipe'=16,'dp'=8,'tensor'=4] {'pipe','tensor'}, use_global_device_ids=true, to_apply=%region_30.31 | all-reduce | flops 128 | bytes 1024 | tf_op jit(solution)/shard_map/psum | solution.py:140
  (724 shorter events, 432.1 us)
Async XLA Ops:
  7.2 272.0 %all-gather.5.cloned.1.call-start = ((), (), s32[]{:S(2)}) async-start(), calls=%async_computation | async-start | bytes 2064384 | tf_op jit(solution)/shard_map/all_gather | solution.py:76
  7.9 274.1 %all-gather.9.cloned.1.call-start = ((), (), s32[]{:S(2)}) async-start(), calls=%async_computation.2 | async-start | bytes 2064384 | tf_op jit(solution)/shard_map/all_gather | solution.py:79
  7.9 8.0 collective-permute-start.2
  15.9 15.6 collective-permute-start.3
  31.5 29.6 %collective-permute-start.4 = (bf16[1,1792,64]{1,2,0:T(8,128)(2,1)S(1)}, bf16[1,1792,64]{1,2,0:T(8,128)(2,1)S(1)}, u32[]{:S(2)}, u32[]{:S(2)}) collective-permute-start(bf16[1,1792,64]{1,2,0:T(8,128)(2,1)S(1)} %collective-permute-done.3), channel_id=1, source_target_pairs={{0,128},{128,0},{32,160},{160,32},{64,192},{192,64},{96,224},{224,... | collective-permute-start | bytes 688136 | tf_op jit(solution)/shard_map/ppermute | solution.py:14
  61.2 32.5 %collective-permute-start.5 = (bf16[1,1792,64]{1,2,0:T(8,128)(2,1)S(1)}, bf16[1,1792,64]{1,2,0:T(8,128)(2,1)S(1)}, u32[]{:S(2)}, u32[]{:S(2)}) collective-permute-start(bf16[1,1792,64]{1,2,0:T(8,128)(2,1)S(1)} %collective-permute-done.4), channel_id=1, source_target_pairs={{0,256},{256,0},{32,288},{288,32},{64,320},{320,64},{96,352},{352,... | collective-permute-start | bytes 688136 | tf_op jit(solution)/shard_map/ppermute | solution.py:14
  94.4 191.4 %all-gather.7.cloned.1.call-start = ((), (), s32[]{:S(2)}) async-start(), calls=%async_computation.1 | async-start | bytes 2064384 | tf_op jit(solution)/shard_map/all_gather | solution.py:78
  95.1 200.1 %all-gather.11.cloned.1.call-start = ((), (), s32[]{:S(2)}) async-start(), calls=%async_computation.3 | async-start | bytes 2064384 | tf_op jit(solution)/shard_map/all_gather | solution.py:81
  95.2 8.7 collective-permute-start.14
  103.9 15.2 collective-permute-start.15
  119.1 24.8 %collective-permute-start.16 = (bf16[1,64,1792]{2,1,0:T(8,128)(2,1)S(1)}, bf16[1,64,1792]{2,1,0:T(8,128)(2,1)S(1)}, u32[]{:S(2)}, u32[]{:S(2)}) collective-permute-start(bf16[1,64,1792]{2,1,0:T(8,128)(2,1)S(1)} %collective-permute-done.15), channel_id=1, source_target_pairs={{0,128},{128,0},{32,160},{160,32},{64,192},{192,64},{96,224},{224,... | collective-permute-start | bytes 688136 | tf_op jit(solution)/shard_map/ppermute | solution.py:14
  143.8 25.3 %collective-permute-start.17 = (bf16[1,64,1792]{2,1,0:T(8,128)(2,1)S(1)}, bf16[1,64,1792]{2,1,0:T(8,128)(2,1)S(1)}, u32[]{:S(2)}, u32[]{:S(2)}) collective-permute-start(bf16[1,64,1792]{2,1,0:T(8,128)(2,1)S(1)} %collective-permute-done.16), channel_id=1, source_target_pairs={{0,256},{256,0},{32,288},{288,32},{64,320},{320,64},{96,352},{352,... | collective-permute-start | bytes 688136 | tf_op jit(solution)/shard_map/ppermute | solution.py:14
  174.6 11.1 collective-permute-start.11
  181.5 7.5 collective-permute-start.7
  185.7 9.9 collective-permute-start.12
  189.0 46.8 %collective-permute-start.8 = (bf16[1,512]{1,0:T(2,128)(2,1)S(1)}, bf16[1,512]{1,0:T(2,128)(2,1)S(1)}, u32[]{:S(2)}, u32[]{:S(2)}) collective-permute-start(bf16[1,512]{1,0:T(2,128)(2,1)S(1)} %collective-permute-done.7), channel_id=1, source_target_pairs={{0,128},{128,0},{32,160},{160,32},{64,192},{192,64},{96,224},{224,... | collective-permute-start | bytes 3080 | tf_op jit(solution)/shard_map/ppermute | solution.py:14
  195.6 53.3 %collective-permute-start.13 = (bf16[1,64,128]{2,1,0:T(8,128)(2,1)S(1)}, bf16[1,64,128]{2,1,0:T(8,128)(2,1)S(1)}, u32[]{:S(2)}, u32[]{:S(2)}) collective-permute-start(bf16[1,64,128]{2,1,0:T(8,128)(2,1)S(1)} %collective-permute-done.12), channel_id=1, source_target_pairs={{0,256},{256,0},{32,288},{288,32},{64,320},{320,64},{96,352},{352,... | collective-permute-start | bytes 49160 | tf_op jit(solution)/shard_map/ppermute | solution.py:14
  235.8 13.0 collective-permute-start.9
  296.0 58.4 %all-reduce.8.cloned.1.call-start = ((), (), s32[]{:S(2)}) async-start(), calls=%async_computation.4 | async-start | bytes 524288 | tf_op jit(solution)/shard_map/while/body/eval_jaxpr/psum | solution.py:44
  378.9 7.6 collective-permute-start.1
  386.4 58.4 %all-reduce.8.cloned.1.call-start = ((), (), s32[]{:S(2)}) async-start(), calls=%async_computation.4 | async-start | bytes 524288 | tf_op jit(solution)/shard_map/while/body/eval_jaxpr/psum | solution.py:44
  465.9 9.9 collective-permute-start
  471.2 8.4 collective-permute-start.1
  479.6 56.0 %all-reduce.8.cloned.1.call-start = ((), (), s32[]{:S(2)}) async-start(), calls=%async_computation.4 | async-start | bytes 524288 | tf_op jit(solution)/shard_map/while/body/eval_jaxpr/psum | solution.py:44
  556.7 8.0 collective-permute-start
  560.1 10.4 collective-permute-start.1
  570.5 55.9 %all-reduce.8.cloned.1.call-start = ((), (), s32[]{:S(2)}) async-start(), calls=%async_computation.4 | async-start | bytes 524288 | tf_op jit(solution)/shard_map/while/body/eval_jaxpr/psum | solution.py:44
  647.5 8.0 collective-permute-start
  650.9 8.3 collective-permute-start.1
  659.3 57.9 %all-reduce.8.cloned.1.call-start = ((), (), s32[]{:S(2)}) async-start(), calls=%async_computation.4 | async-start | bytes 524288 | tf_op jit(solution)/shard_map/while/body/eval_jaxpr/psum | solution.py:44
  738.3 8.0 collective-permute-start
  741.7 8.3 collective-permute-start.1
  750.0 57.6 %all-reduce.8.cloned.1.call-start = ((), (), s32[]{:S(2)}) async-start(), calls=%async_computation.4 | async-start | bytes 524288 | tf_op jit(solution)/shard_map/while/body/eval_jaxpr/psum | solution.py:44
  828.7 8.0 collective-permute-start
  832.2 8.3 collective-permute-start.1
  840.5 58.0 %all-reduce.8.cloned.1.call-start = ((), (), s32[]{:S(2)}) async-start(), calls=%async_computation.4 | async-start | bytes 524288 | tf_op jit(solution)/shard_map/while/body/eval_jaxpr/psum | solution.py:44
  919.6 8.0 collective-permute-start
  923.0 8.3 collective-permute-start.1
  931.4 58.8 %all-reduce.8.cloned.1.call-start = ((), (), s32[]{:S(2)}) async-start(), calls=%async_computation.4 | async-start | bytes 524288 | tf_op jit(solution)/shard_map/while/body/eval_jaxpr/psum | solution.py:44
  1011.3 8.0 collective-permute-start
  1014.7 8.3 collective-permute-start.1
  1023.1 60.0 %all-reduce.8.cloned.1.call-start = ((), (), s32[]{:S(2)}) async-start(), calls=%async_computation.4 | async-start | bytes 524288 | tf_op jit(solution)/shard_map/while/body/eval_jaxpr/psum | solution.py:44
  1104.1 8.0 collective-permute-start
  1107.5 8.3 collective-permute-start.1
  1115.9 59.5 %all-reduce.8.cloned.1.call-start = ((), (), s32[]{:S(2)}) async-start(), calls=%async_computation.4 | async-start | bytes 524288 | tf_op jit(solution)/shard_map/while/body/eval_jaxpr/psum | solution.py:44
  1196.4 8.0 collective-permute-start
  1199.9 8.3 collective-permute-start.1
  1208.2 58.4 %all-reduce.8.cloned.1.call-start = ((), (), s32[]{:S(2)}) async-start(), calls=%async_computation.4 | async-start | bytes 524288 | tf_op jit(solution)/shard_map/while/body/eval_jaxpr/psum | solution.py:44
  1287.7 8.0 collective-permute-start
  1291.2 8.3 collective-permute-start.1
  1299.5 57.6 %all-reduce.8.cloned.1.call-start = ((), (), s32[]{:S(2)}) async-start(), calls=%async_computation.4 | async-start | bytes 524288 | tf_op jit(solution)/shard_map/while/body/eval_jaxpr/psum | solution.py:44
  1378.2 8.0 collective-permute-start
  1381.6 8.3 collective-permute-start.1
  1390.0 57.6 %all-reduce.8.cloned.1.call-start = ((), (), s32[]{:S(2)}) async-start(), calls=%async_computation.4 | async-start | bytes 524288 | tf_op jit(solution)/shard_map/while/body/eval_jaxpr/psum | solution.py:44
  1468.7 8.0 collective-permute-start
  1472.1 8.3 collective-permute-start.1
  1480.4 57.6 %all-reduce.8.cloned.1.call-start = ((), (), s32[]{:S(2)}) async-start(), calls=%async_computation.4 | async-start | bytes 524288 | tf_op jit(solution)/shard_map/while/body/eval_jaxpr/psum | solution.py:44
  1559.1 8.0 collective-permute-start
  1562.6 10.4 collective-permute-start.1
  1572.9 55.9 %all-reduce.8.cloned.1.call-start = ((), (), s32[]{:S(2)}) async-start(), calls=%async_computation.4 | async-start | bytes 524288 | tf_op jit(solution)/shard_map/while/body/eval_jaxpr/psum | solution.py:44
  1649.9 9.9 collective-permute-start
  1655.2 8.3 collective-permute-start.1
  1663.6 55.7 %all-reduce.8.cloned.1.call-start = ((), (), s32[]{:S(2)}) async-start(), calls=%async_computation.4 | async-start | bytes 524288 | tf_op jit(solution)/shard_map/while/body/eval_jaxpr/psum | solution.py:44
  1743.8 7.6 collective-permute-start.1
  (40 other events, 70.4 us)
Sparse Core Ops, SparseCore 0:
  11.2 71.8 all-gather.4
  94.5 62.6 all-gather.8
  160.4 66.4 all-gather.6
  229.9 65.2 all-gather.10
  299.5 54.8 all-reduce.7
  389.9 54.8 all-reduce.7
  483.4 52.1 all-reduce.7
  574.3 52.0 all-reduce.7
  663.1 54.1 all-reduce.7
  753.5 54.1 all-reduce.7
  844.3 54.1 all-reduce.7
  934.9 55.3 all-reduce.7
  1026.9 56.1 all-reduce.7
  1119.3 56.0 all-reduce.7
  1211.7 54.9 all-reduce.7
  1303.0 54.1 all-reduce.7
  1393.5 54.1 all-reduce.7
  1483.9 54.1 all-reduce.7
  1576.7 52.0 all-reduce.7
  1667.5 51.7 all-reduce.7
where the time goes:
time: 1870 us
  waiting for transfers between devices  1080 us (58%)
  blocking collectives  341 us (18%)
  other arithmetic  173 us (9%)
  starting transfers between devices  157 us (8%)
  matrix products  50.7 us (3%)
  local copies, waits for them, and re-layouts  48 us (3%)
    psum x16, waiting for transfers between devices, run_layer(): whole = lax.psum(part, 'tensor')  850 us
    psum x16, blocking collectives, run_layer(): lax.psum(jnp.dot(query, keys.T, preferred_element_type=jnp.float32), 'ten...  170 us
    ppermute x16, waiting for transfers between devices, from_partner(): return lax.ppermute(block, axis, route)  121 us
    psum x1, blocking collectives, body(): scores = lax.psum(exits, ('pipe', 'tensor'))  107 us
    ppermute x32, waiting for transfers between devices, from_behind(): return lax.ppermute(block, axis, route)  94.8 us
    ppermute x16, starting transfers between devices, from_partner(): return lax.ppermute(block, axis, route)  81.4 us
    ppermute x32, starting transfers between devices, from_behind(): return lax.ppermute(block, axis, route)  75.6 us
    scatter x32, other arithmetic, advance(): kept = kept.at[side, index].set(jnp.where(active, latent, previous))  72.2 us
  transfers between devices with their start and end apart: 68, of which 60 were waited for; matrix products, arithmetic and copies ran while one was open for 4% of the time, Pallas kernels for 0%

commit v1 on v0

v1 whole, which is shorter than its diff:
```python
import functools

import jax
import jax.numpy as jnp
from jax import lax
from jax.experimental import pallas as pl
from jax.experimental.pallas import tpu as pltpu
from jax.sharding import PartitionSpec as P

F32 = jnp.float32
BF16 = jnp.bfloat16
MESH = pl.DeviceIdType.MESH


def nt_dot(a, b):
    return lax.dot_general(a, b, (((1,), (1,)), ((), ())), preferred_element_type=F32)


def dot(a, b):
    return jnp.dot(a, b, preferred_element_type=F32)


def kernel(
    n, nd,
    x_hbm, len_ref, wd_hbm, wq_hbm, wo_hbm, gain_ref, read_ref,
    lat_out, score_out,
    xv, wd, wq, ring, csend, crecv, g, gnear, p0send, p0recv, acc, p2, near2,
    mixed, latv, lat, sin, sout, fin, maskv, dummy,
    loc, asem, qsem, ups, upr, dns, dnr, cs, cr, d1s, d1r, d2s, d2r,
    nx, psem, ms, mr, ex, ssem, lats, latr, fs, fr,
):
    seq = latv.shape[0]
    width = latv.shape[1]
    half = width // 2
    rows = wo_hbm.shape[0]
    quarter = wq_hbm.shape[1]
    ny = nd // 2
    up_steps = n // 2
    low = up_steps - 2
    last = n - 1

    l = lax.axis_index("pipe")
    d = lax.axis_index("dp")
    t = lax.axis_index("tensor")
    y, xh = d // 2, d % 2
    e, c = t // 2, t % 2

    def tensor_of(x_low, core):
        return 2 * x_low + core

    gather_peers = [(l, (d + k) % nd, t) for k in range(1, nd)]
    cut_peers = [(e, 1 - c), (1 - e, c), (1 - e, 1 - c)]
    core_peer = (l, d, tensor_of(e, 1 - c))
    y_peers = [(l, ((y + k) % ny) * 2 + xh, t) for k in range(1, ny)]
    x_peers = [
        (l, 2 * y + 1 - xh, t),
        (l, d, tensor_of(1 - e, c)),
        (l, 2 * y + 1 - xh, tensor_of(1 - e, c)),
    ]
    above = ((l + 1) % n, d, t)
    below = ((l + n - 1) % n, d, t)
    mirror = [(last - l, d, tensor_of(k, c)) for k in range(2)]

    def send(src, dst, ssem_, rsem_, device):
        pltpu.make_async_remote_copy(
            src_ref=src, dst_ref=dst, send_sem=ssem_, recv_sem=rsem_,
            device_id=device, device_id_type=MESH,
        ).start()

    def wait_for(ref, sem):
        pltpu.make_async_copy(ref, ref, sem).wait()

    own_rows = pl.ds(pl.multiple_of(d * rows, rows), rows)
    pair_rows = pl.ds(pl.multiple_of(xh * rows, rows), rows)
    own_cols = pl.ds(pl.multiple_of(e * quarter, quarter), quarter)
    query_cols = pl.ds(pl.multiple_of(t * quarter, quarter), quarter)

    local = [
        pltpu.make_async_copy(wd_hbm, wd.at[own_rows], loc.at[0]),
        pltpu.make_async_copy(wo_hbm, ring.at[l], loc.at[1]),
        pltpu.make_async_copy(wq_hbm, wq.at[y, pair_rows, query_cols], loc.at[2]),
        pltpu.make_async_copy(x_hbm, xv, loc.at[3]),
    ]
    for copy in local:
        copy.start()

    barrier = pltpu.get_barrier_semaphore()

    def greet(device):
        pl.semaphore_signal(barrier, inc=1, device_id=device, device_id_type=MESH)

    greeted = gather_peers + [(l, d, tensor_of(*p)) for p in cut_peers]
    greeted += [x_peers[2], above, below] + mirror
    for device in greeted:
        greet(device)

    @pl.when(l == last)
    def _():
        def one(p, carry):
            greet((p, d, tensor_of(0, c)))
            greet((p, d, tensor_of(1, c)))
            return carry
        lax.fori_loop(0, last, one, 0)

    @pl.when(l < last)
    def _():
        greet((last, d, tensor_of(0, c)))
        greet((last, d, tensor_of(1, c)))

    pl.semaphore_wait(barrier, len(greeted) + jnp.where(l == last, 2 * last, 2))

    for copy in local:
        copy.wait()

    for device in gather_peers:
        send(wd.at[own_rows], wd.at[own_rows], asem.at[0], asem.at[1], device)

    def up_send(s):
        @pl.when((s <= l) & (l < last) & (s < up_steps))
        def _():
            j = l - s
            send(ring.at[j], ring.at[j], ups.at[s], upr.at[s], above)

    def down_valid(who, s):
        return (s < up_steps - 1) & ((who + s <= low) | (who + s >= n))

    def down_send(s):
        @pl.when(down_valid(l, s))
        def _():
            j = (l + s) % n
            send(ring.at[j], ring.at[j], dns.at[s], dnr.at[s], below)

    behind = (l + 1) % n

    def ring_step(s):
        @pl.when(s < l)
        def _():
            wait_for(ring.at[l - 1 - s], upr.at[s])
            up_send_next(s)

        @pl.when(down_valid(behind, s))
        def _():
            wait_for(ring.at[(l + 1 + s) % n], dnr.at[s])
            down_send_next(s)

    def up_send_next(s):
        @pl.when(s + 1 < up_steps)
        def _():
            up_send(s + 1)

    def down_send_next(s):
        @pl.when(s + 1 < up_steps - 1)
        def _():
            down_send(s + 1)

    up_send(0)
    down_send(0)

    def spread_first(ref, cols, s_sem, r_sem):
        for device in y_peers:
            piece = ref.at[y, pair_rows, cols]
            send(piece, piece, s_sem, r_sem, device)

    def wait_first(sem):
        if ny > 1:
            wait_for(dummy.at[pl.ds(0, ny - 1)], sem)

    def spread_second(ref, cols, s_sem, r_sem):
        for device in x_peers:
            piece = ref.at[:, pair_rows, cols]
            send(piece, piece, s_sem, r_sem, device)

    def wait_second(sem):
        wait_for(dummy, sem)

    spread_first(wq, query_cols, qsem.at[0], qsem.at[1])

    def cut_send(j, part):
        for b in range(4):
            csend[j, b] = part[:, b * quarter:(b + 1) * quarter].astype(BF16)
        for x_low, core in cut_peers:
            send(
                csend.at[j, 2 * core + x_low], crecv.at[j, t], cs.at[j], cr.at[j],
                (l, d, tensor_of(x_low, core)),
            )

    def cut_sum(j):
        wait_for(dummy.at[pl.ds(0, 3)], cr.at[j])
        crecv[j, t] = csend[j, 2 * c + e]
        total = crecv[j, 0].astype(F32)
        for k in range(1, 4):
            total = total + crecv[j, k].astype(F32)
        g[j, y, pair_rows, own_cols] = total.astype(BF16)
        spread_first(g.at[j], own_cols, d1s.at[j], d1r.at[j])

    def pass_on(j):
        wait_first(d1r.at[j])
        spread_second(g.at[j], own_cols, d2s.at[j], d2r.at[j])

    seen = jnp.sum(ring[l].astype(F32) * read_ref[...].astype(F32), axis=1, keepdims=True)
    cut_send(l, jnp.broadcast_to(seen, (rows, width)))

    early = min(3, up_steps)
    for s in range(early):
        ring_step(s)
        if s == 0:
            cut_sum(l)
            wait_first(qsem.at[1])
            spread_second(wq, query_cols, qsem.at[2], qsem.at[3])
        if s == 1:
            pass_on(l)
            wait_second(qsem.at[3])
            for k in range(2):
                cols = pl.ds(pl.multiple_of((2 * k + c) * quarter, quarter), quarter)
                piece = wq.at[:, :, cols]
                send(piece, piece, qsem.at[4], qsem.at[5], core_peer)

    i0 = lax.broadcasted_iota(jnp.int32, (seq, seq), 0)
    i1 = lax.broadcasted_iota(jnp.int32, (seq, seq), 1)
    doc0 = jnp.zeros((seq, seq), jnp.int32)
    doc1 = jnp.zeros((seq, seq), jnp.int32)
    end = jnp.int32(0)
    for k in range(len_ref.shape[1]):
        end = end + len_ref[e, k]
        doc0 = doc0 + (i0 >= end).astype(jnp.int32)
        doc1 = doc1 + (i1 >= end).astype(jnp.int32)
    maskv[...] = ((doc0 == doc1) & (i1 <= i0)).astype(F32)

    wait_for(wd.at[pl.ds(0, (nd - 1) * rows)], asem.at[1])
    head = jnp.sum(xv[...].astype(F32) * read_ref[...].astype(F32), axis=1, keepdims=True)
    for core in range(2):
        part = nt_dot(xv[...], wd[core * half:(core + 1) * half])
        for x_low in range(2):
            b = 2 * core + x_low
            p0send[b, :, 0:half] = part[x_low * seq:(x_low + 1) * seq]
            p0send[b, :, half:half + 128] = jnp.broadcast_to(
                head[x_low * seq:(x_low + 1) * seq], (seq, 128)
            )
    for x_low, core in cut_peers:
        send(
            p0send.at[2 * core + x_low], p0recv.at[t], psem.at[0], psem.at[1],
            (l, d, tensor_of(x_low, core)),
        )

    def items(s, do):
        @pl.when((s >= 0) & (s < up_steps) & (s < l))
        def _():
            do(l - 1 - s)

        @pl.when((s >= 0) & down_valid(behind, s) & ((l + 1 + s) % n < l))
        def _():
            do((l + 1 + s) % n)

    def product(j):
        cut_send(j, nt_dot(ring[j], wd[...]))

    def prepare(s, carry):
        @pl.when((s >= early) & (s < up_steps))
        def _():
            ring_step(s)
        items(s, product)
        items(s - 1, cut_sum)
        items(s - 2, pass_on)
        return carry

    lax.fori_loop(0, up_steps + 2, prepare, 0)

    @pl.when(l > 0)
    def _():
        wait_second(d2r.at[l - 1])
        send(g.at[l - 1], gnear, nx.at[0], nx.at[1], core_peer)

    wait_for(p0recv.at[pl.ds(0, 3)], psem.at[1])
    p0recv[t] = p0send[2 * c + e]
    whole = p0recv[0]
    for k in range(1, 4):
        whole = whole + p0recv[k]
    acc[...] = whole[:, 0:half]
    s0 = lax.broadcasted_iota(jnp.int32, (seq, 128), 0)
    s1 = lax.broadcasted_iota(jnp.int32, (seq, 128), 1)
    diagonal = (s0 == s1).astype(F32)

    def as_row(columns):
        row = jnp.sum(columns * diagonal, axis=0, keepdims=True)
        return jnp.broadcast_to(row, (8, 128))

    @pl.when(l == 0)
    def _():
        sin[...] = as_row(whole[:, half:half + 128])

    def mixed_in(j):
        wait_for(mixed.at[j], mr.at[j])

        @pl.when(l < last)
        def _():
            send(mixed.at[j], mixed.at[j], ms.at[j], mr.at[j], above)

    def far(j, carry):
        mixed_in(j)
        wait_second(d2r.at[j])
        acc[...] += dot(mixed[j], g[j].reshape(width, half))
        return carry

    lax.fori_loop(0, l - 1, far, 0)
    p2[c] = acc[...]
    send(p2.at[c], p2.at[c], ex.at[0], ex.at[1], core_peer)
    wait_second(d2r.at[l])
    wait_for(wq.at[:, :, pl.ds(0, half)], qsem.at[5])
    wait_for(p2.at[1 - c], ex.at[1])

    @pl.when(l == 0)
    def _():
        near2[...] = jnp.zeros_like(near2)

    @pl.when(l > 0)
    def _():
        wait_for(gnear, nx.at[1])
        mixed_in(l - 1)
        got = mixed[l - 1]
        near2[c] = dot(got, g[l - 1].reshape(width, half))
        near2[1 - c] = dot(got, gnear[...].reshape(width, half))

    part = jnp.concatenate([p2[0] + near2[0], p2[1] + near2[1]], axis=1)
    scale = lax.rsqrt(jnp.mean(part * part, axis=1, keepdims=True) + 1e-06)
    latent = (part * scale * gain_ref[...].astype(F32)).astype(BF16)
    query = dot(latent, wq[...].reshape(width, width)).astype(BF16)
    logits = nt_dot(query, latent) * (1.0 / float(width) ** 0.5)
    logits = jnp.where(maskv[...] > 0.5, logits, -1e30)
    top = jnp.max(logits, axis=1, keepdims=True)
    raised = jnp.exp(logits - top)
    weights = (raised / jnp.sum(raised, axis=1, keepdims=True)).astype(BF16)
    mixed[l] = dot(weights, latent).astype(BF16)

    @pl.when(l < last)
    def _():
        send(mixed.at[l], mixed.at[l], ms.at[l], mr.at[l], above)

    latv[...] = latent

    @pl.when(e == 0)
    def _():
        lat[0] = latent
        send(latv, lat.at[0], lats.at[0], latr.at[0], (l, d, tensor_of(1, c)))

    @pl.when(e == 1)
    def _():
        for k in range(2):
            send(latv, lat.at[1], lats.at[k], latr.at[1], mirror[k])

    value = as_row(dot(mixed[l], g[l].reshape(width, half)[:, 0:128]))

    @pl.when(l > 0)
    def _():
        wait_for(sin, ssem.at[1])

    sout[...] = sin[...] + value

    @pl.when(l < last)
    def _():
        send(sout, sin, ssem.at[0], ssem.at[1], above)
        wait_for(fin.at[0], fr.at[0])
        wait_for(fin.at[1], fr.at[1])

    @pl.when(l == last)
    def _():
        fin[e] = sout[...]
        send(sout, fin.at[e], fs.at[last], fr.at[e], (l, d, tensor_of(1 - e, c)))

        def one(p, carry):
            for k in range(2):
                send(sout, fin.at[e], fs.at[p + k * n], fr.at[e], (p, d, tensor_of(k, c)))
            return carry
        lax.fori_loop(0, last, one, 0)
        wait_for(fin.at[1 - e], fr.at[1 - e])

    @pl.when(e == 1)
    def _():
        wait_for(lat.at[0], latr.at[0])

    wait_for(lat.at[1], latr.at[1])
    lat_out[...] = lat[...]
    score_out[0:1, :] = fin[0, 0:1, 0:seq]
    score_out[1:2, :] = fin[1, 0:1, 0:seq]

    wait_for(wd.at[pl.ds(0, (nd - 1) * rows)], asem.at[0])
    wait_first(qsem.at[0])
    wait_second(qsem.at[2])
    wait_for(wq.at[:, :, pl.ds(0, half)], qsem.at[4])
    wait_for(p0recv.at[pl.ds(0, 3)], psem.at[0])
    wait_for(p2.at[c], ex.at[0])

    def ring_left(s, carry):
        @pl.when((s <= l) & (l < last))
        def _():
            wait_for(ring.at[l], ups.at[s])

        @pl.when(down_valid(l, s))
        def _():
            wait_for(ring.at[l], dns.at[s])
        return carry

    lax.fori_loop(0, up_steps, ring_left, 0)

    def item_left(j, carry):
        wait_for(dummy.at[pl.ds(0, 3)], cs.at[j])
        wait_first(d1s.at[j])
        wait_second(d2s.at[j])

        @pl.when(l < last)
        def _():
            wait_for(mixed.at[j], ms.at[j])
        return carry

    lax.fori_loop(0, l + 1, item_left, 0)

    @pl.when(l > 0)
    def _():
        wait_for(gnear, nx.at[0])

    wait_for(latv, lats.at[0])

    @pl.when(e == 1)
    def _():
        wait_for(latv, lats.at[1])

    @pl.when(l < last)
    def _():
        wait_for(sout, ssem.at[0])

    @pl.when(l == last)
    def _():
        wait_for(sout, fs.at[last])

        def one(p, carry):
            wait_for(sout, fs.at[p])
            wait_for(sout, fs.at[p + n])
            return carry
        lax.fori_loop(0, last, one, 0)


def body(inputs, lengths, w_down, w_query, w_out, gain_latent, readout):
    n = lax.axis_size("pipe")
    nd = lax.axis_size("dp")
    _, _, seq, feats = inputs.shape
    rows = w_query.shape[1]
    quarter = w_query.shape[2]
    width = rows * nd
    half = width // 2
    up_steps = n // 2
    dma = pltpu.SemaphoreType.DMA
    hbm = pl.BlockSpec(memory_space=pl.ANY)
    vmem = pl.BlockSpec(memory_space=pltpu.VMEM)
    latents, scores = pl.pallas_call(
        functools.partial(kernel, n, nd),
        out_shape=(
            jax.ShapeDtypeStruct((2, seq, width), BF16),
            jax.ShapeDtypeStruct((2, seq), F32),
        ),
        in_specs=[hbm, pl.BlockSpec(memory_space=pltpu.SMEM), hbm, hbm, hbm, vmem, vmem],
        out_specs=(vmem, vmem),
        scratch_shapes=[
            pltpu.VMEM((2 * seq, feats), BF16),
            pltpu.VMEM((width, feats), BF16),
            pltpu.VMEM((nd // 2, 2 * rows, width), BF16),
            pltpu.VMEM((n, rows, feats), BF16),
            pltpu.VMEM((n, 4, rows, quarter), BF16),
            pltpu.VMEM((n, 4, rows, quarter), BF16),
            pltpu.VMEM((n, nd // 2, 2 * rows, half), BF16),
            pltpu.VMEM((nd // 2, 2 * rows, half), BF16),
            pltpu.VMEM((4, seq, half + 128), F32),
            pltpu.VMEM((4, seq, half + 128), F32),
            pltpu.VMEM((seq, half), F32),
            pltpu.VMEM((2, seq, half), F32),
            pltpu.VMEM((2, seq, half), F32),
            pltpu.VMEM((n, seq, width), BF16),
            pltpu.VMEM((seq, width), BF16),
            pltpu.VMEM((2, seq, width), BF16),
            pltpu.VMEM((8, 128), F32),
            pltpu.VMEM((8, 128), F32),
            pltpu.VMEM((2, 8, 128), F32),
            pltpu.VMEM((seq, seq), F32),
            pltpu.VMEM((3 * max(nd // 2, 1), rows, quarter), BF16),
            dma((4,)),
            dma((2,)),
            dma((6,)),
            dma((up_steps,)),
            dma((up_steps,)),
            dma((up_steps,)),
            dma((up_steps,)),
            dma((n,)),
            dma((n,)),
            dma((n,)),
            dma((n,)),
            dma((n,)),
            dma((n,)),
            dma((2,)),
            dma((2,)),
            dma((n,)),
            dma((n,)),
            dma((2,)),
            dma((2,)),
            dma((2,)),
            dma((2,)),
            dma((2 * n,)),
            dma((2,)),
        ],
        compiler_params=pltpu.CompilerParams(
            collective_id=0, has_side_effects=True, vmem_limit_bytes=40 * 1024 * 1024
        ),
    )(
        inputs.reshape(2 * seq, feats),
        lengths.reshape(2, lengths.shape[2]),
        w_down[0].T,
        w_query[0],
        w_out[0],
        gain_latent,
        readout.reshape(1, feats),
    )
    return latents.reshape(1, 2, 1, seq, width), scores.reshape(2, 1, seq)


def solution(mesh):
    in_specs = (
        P(None, "dp", None, "tensor"),
        P(None, "dp", None),
        P("pipe", "tensor", "dp"),
        P("pipe", "dp", "tensor"),
        P("pipe", "dp", "tensor"),
        P("pipe", None),
        P("tensor"),
    )
    out_specs = (P("pipe", None, "dp", None, None), P(None, "dp", None))
    return jax.shard_map(body, mesh=mesh, in_specs=in_specs, out_specs=out_specs, check_vma=False)
```

time: 1870 us -> 174 us (0.09)
  waiting for transfers between devices: 1080 us -> 0 us
  blocking collectives: 341 us -> 0 us
  other arithmetic: 173 us -> 0 us
  Pallas kernels: 0 us -> 167 us
  starting transfers between devices: 157 us -> 0 us
  matrix products: 50.7 us -> 0 us
  local copies, waits for them, and re-layouts: 48 us -> 4.83 us
    psum x16 -> x0, waiting for transfers between devices: 850 us -> none  [run_layer(): whole = lax.psum(part, 'tensor')]
    psum x17 -> x0, blocking collectives: 277 us -> none  [the longest x16 170 us: run_layer(): lax.psum(jnp.dot(query, keys.T, preferred_element_type=jnp.float32), 'ten...]
    ppermute x48 -> x0, waiting for transfers between devices: 216 us -> none  [the longest x16 121 us: from_partner(): return lax.ppermute(block, axis, route)]
    pallas_call x0 -> x1, Pallas kernels: none -> 167 us  [body(): pl.pallas_call(functools.partial(kernel, n, nd), out_shape=(jax.ShapeDtyp...]
    ppermute x48 -> x0, starting transfers between devices: 157 us -> none  [the longest x16 81.4 us: from_partner(): return lax.ppermute(block, axis, route)]
    scatter x32 -> x0, other arithmetic: 72.2 us -> none  [advance(): kept = kept.at[side, index].set(jnp.where(active, latent, previous))]
    all_gather x2 -> x0, blocking collectives: 63.9 us -> none  [the longest x1 33.6 us: body(): lax.all_gather(w_query, 'dp', axis=1, tiled=True)]
    dot_general x68 -> x0, matrix products: 50.7 us -> none  [the longest x32 37.5 us: run_layer(): jnp.dot(query, keys.T, preferred_element_type=jnp.float32)]
  transfers between devices with their start and end apart: 68 -> 0, of which waited for: 60 -> 0; matrix products, arithmetic and copies ran while one was open for 4% -> 0% of each run, Pallas kernels for 0% -> 0%
where the time goes in v1:
time: 174 us; the launch traced here: 172 us
  Pallas kernels  167 us (96%)
  local copies, waits for them, and re-layouts  4.83 us (3%)
    pallas_call x1, Pallas kernels, body(): pl.pallas_call(functools.partial(kernel, n, nd), out_shape=(jax.ShapeDtyp...  167 us
    unnamed x14, local copies, waits for them, and re-layouts  4.12 us

profile of v1, /device:TPU:1, one launch (start us, length us, event | category | flops | bytes accessed | tf_op | source)
XLA Modules:
  0.0 172.4 jit_solution(17034891263488141612)
XLA Ops:
  0.6 0.0 copy-start.3
  0.6 0.0 copy-start.4
  0.7 0.0 copy-start.5
  0.7 0.7 reshape.21.read_ref
  1.4 0.0 copy-done.3
  1.4 0.0 copy-done.4
  1.4 0.0 copy-done.5
  1.4 0.0 copy-start
  1.4 1.0 copy-done
  2.4 0.0 copy-start.1
  2.4 0.9 copy-done.1
  3.4 0.0 copy-start.2
  3.4 0.9 copy-done.2
  4.3 166.9 %shard_map.86 = (bf16[2,64,512]{2,1,0:T(8,128)(2,1)S(1)}, f32[2,64]{1,0:T(2,128)S(1)}) custom-call(bf16[128,1792]{1,0:T(8,128)(2,1)S(1)} %bitcast.13, s32[2,4]{1,0:T(2,128)S(1)} %bitcast.18, bf16[64,1792]{1,0:T(8,128)(2,1)S(1)} %bitcast.14, bf16[64,128]{1,0:T(8,128)(2,1)S(1)} %bitcast.17, bf16[64,1792]{1,0:T(8,128)(2,1)S(1)} %bitcast.15, ...), custom_call_target="tpu_custom_call" | custom-call | tf_op jit(solution)/shard_map/pallas_call | solution.py:453
  171.2 0.7 copy.13
  171.9 0.6 copy.14
Async XLA Ops:
  0.6 0.7 copy-start.3
  0.6 0.7 copy-start.4
  0.7 0.7 copy-start.5
  1.4 1.0 copy-start
  2.4 0.9 copy-start.1
  3.4 0.9 copy-start.2

commit v2 on v1

--- a/solution.py
+++ b/solution.py
@@ -27,7 +27,7 @@
     xv, wd, wq, ring, csend, crecv, g, gnear, p0send, p0recv, acc, p2, near2,
     mixed, latv, lat, sin, sout, fin, maskv, dummy,
     loc, asem, qsem, ups, upr, dns, dnr, cs, cr, d1s, d1r, d2s, d2r,
-    nx, psem, ms, mr, ex, ssem, lats, latr, fs, fr,
+    nx, psem, ms, mc, mr, ex, ssem, lats, latr, fs, fr,
 ):
     seq = latv.shape[0]
     width = latv.shape[1]
@@ -48,7 +48,6 @@
     def tensor_of(x_low, core):
         return 2 * x_low + core
 
-    gather_peers = [(l, (d + k) % nd, t) for k in range(1, nd)]
     cut_peers = [(e, 1 - c), (1 - e, c), (1 - e, 1 - c)]
     core_peer = (l, d, tensor_of(e, 1 - c))
     y_peers = [(l, ((y + k) % ny) * 2 + xh, t) for k in range(1, ny)]
@@ -59,7 +58,9 @@
     ]
     above = ((l + 1) % n, d, t)
     below = ((l + n - 1) % n, d, t)
-    mirror = [(last - l, d, tensor_of(k, c)) for k in range(2)]
+    above_two = ((l + 2) % n, d, t)
+    below_two = ((l + n - 2) % n, d, t)
+    mirror = [(last - l, d, k) for k in range(4)]
 
     def send(src, dst, ssem_, rsem_, device):
         pltpu.make_async_remote_copy(
@@ -89,31 +90,26 @@
     def greet(device):
         pl.semaphore_signal(barrier, inc=1, device_id=device, device_id_type=MESH)
 
-    greeted = gather_peers + [(l, d, tensor_of(*p)) for p in cut_peers]
-    greeted += [x_peers[2], above, below] + mirror
+    greeted = x_peers + y_peers + [core_peer, (l, d, tensor_of(1 - e, 1 - c))]
+    greeted += [above, below, above_two, below_two]
     for device in greeted:
         greet(device)
 
-    @pl.when(l == last)
-    def _():
-        def one(p, carry):
-            greet((p, d, tensor_of(0, c)))
-            greet((p, d, tensor_of(1, c)))
-            return carry
-        lax.fori_loop(0, last, one, 0)
-
-    @pl.when(l < last)
-    def _():
-        greet((last, d, tensor_of(0, c)))
-        greet((last, d, tensor_of(1, c)))
-
-    pl.semaphore_wait(barrier, len(greeted) + jnp.where(l == last, 2 * last, 2))
+    greet((last - l, d, tensor_of(1, 0)))
+    pl.semaphore_wait(barrier, len(greeted) + jnp.where(t == tensor_of(1, 0), 4, 0))
 
     for copy in local:
         copy.wait()
 
-    for device in gather_peers:
-        send(wd.at[own_rows], wd.at[own_rows], asem.at[0], asem.at[1], device)
+    far_rows = pl.ds(pl.multiple_of((2 * y + 1 - xh) * rows, rows), rows)
+    y_bytes = wd.at[pl.ds(0, (ny - 1) * rows)]
+
+    def gather_y(cols, s_sem, r_sem):
+        for device in y_peers:
+            send(wd.at[cols], wd.at[cols], s_sem, r_sem, device)
+
+    send(wd.at[own_rows], wd.at[own_rows], asem.at[0], asem.at[1], x_peers[0])
+    gather_y(own_rows, asem.at[2], asem.at[3])
 
     def up_send(s):
         @pl.when((s <= l) & (l < last) & (s < up_steps))
@@ -157,21 +153,20 @@
     down_send(0)
 
     def spread_first(ref, cols, s_sem, r_sem):
-        for device in y_peers:
+        for device in x_peers:
             piece = ref.at[y, pair_rows, cols]
             send(piece, piece, s_sem, r_sem, device)
 
     def wait_first(sem):
+        wait_for(dummy.at[pl.ds(0, 3)], sem)
+
+    def spread_second(piece, s_sem, r_sem):
+        for device in y_peers:
+            send(piece, piece, s_sem, r_sem, device)
+
+    def wait_second(sem):
         if ny > 1:
-            wait_for(dummy.at[pl.ds(0, ny - 1)], sem)
-
-    def spread_second(ref, cols, s_sem, r_sem):
-        for device in x_peers:
-            piece = ref.at[:, pair_rows, cols]
-            send(piece, piece, s_sem, r_sem, device)
-
-    def wait_second(sem):
-        wait_for(dummy, sem)
+            wait_for(dummy, sem)
 
     spread_first(wq, query_cols, qsem.at[0], qsem.at[1])
 
@@ -195,7 +190,7 @@
 
     def pass_on(j):
         wait_first(d1r.at[j])
-        spread_second(g.at[j], own_cols, d2s.at[j], d2r.at[j])
+        spread_second(g.at[j, y], d2s.at[j], d2r.at[j])
 
     seen = jnp.sum(ring[l].astype(F32) * read_ref[...].astype(F32), axis=1, keepdims=True)
     cut_send(l, jnp.broadcast_to(seen, (rows, width)))
@@ -206,14 +201,21 @@
         if s == 0:
             cut_sum(l)
             wait_first(qsem.at[1])
-            spread_second(wq, query_cols, qsem.at[2], qsem.at[3])
+            for k in range(2):
+                cols = pl.ds(pl.multiple_of((2 * k + c) * quarter, quarter), quarter)
+                spread_second(wq.at[y, :, cols], qsem.at[2], qsem.at[3])
+            wait_for(wd.at[far_rows], asem.at[1])
+            gather_y(far_rows, asem.at[4], asem.at[5])
         if s == 1:
             pass_on(l)
             wait_second(qsem.at[3])
-            for k in range(2):
-                cols = pl.ds(pl.multiple_of((2 * k + c) * quarter, quarter), quarter)
-                piece = wq.at[:, :, cols]
-                send(piece, piece, qsem.at[4], qsem.at[5], core_peer)
+
+            @pl.when(c == 1)
+            def _():
+                for k in range(2):
+                    cols = pl.ds((2 * k + 1) * quarter, quarter)
+                    piece = wq.at[:, :, cols]
+                    send(piece, piece, qsem.at[4], qsem.at[5], core_peer)
 
     i0 = lax.broadcasted_iota(jnp.int32, (seq, seq), 0)
     i1 = lax.broadcasted_iota(jnp.int32, (seq, seq), 1)
@@ -226,7 +228,9 @@
         doc1 = doc1 + (i1 >= end).astype(jnp.int32)
     maskv[...] = ((doc0 == doc1) & (i1 <= i0)).astype(F32)
 
-    wait_for(wd.at[pl.ds(0, (nd - 1) * rows)], asem.at[1])
+    if ny > 1:
+        wait_for(y_bytes, asem.at[3])
+        wait_for(y_bytes, asem.at[5])
     head = jnp.sum(xv[...].astype(F32) * read_ref[...].astype(F32), axis=1, keepdims=True)
     for core in range(2):
         part = nt_dot(xv[...], wd[core * half:(core + 1) * half])
@@ -263,12 +267,15 @@
         items(s - 2, pass_on)
         return carry
 
-    lax.fori_loop(0, up_steps + 2, prepare, 0)
-
-    @pl.when(l > 0)
-    def _():
-        wait_second(d2r.at[l - 1])
-        send(g.at[l - 1], gnear, nx.at[0], nx.at[1], core_peer)
+    ready = jnp.minimum(l, up_steps) + 2
+    lax.fori_loop(0, ready, prepare, 0)
+
+    close = 3
+    for k in range(close):
+        @pl.when((l > k) & (c == 1))
+        def _():
+            wait_second(d2r.at[l - 1 - k])
+            send(g.at[l - 1 - k], gnear.at[k], nx.at[k], nx.at[close + k], core_peer)
 
     wait_for(p0recv.at[pl.ds(0, 3)], psem.at[1])
     p0recv[t] = p0send[2 * c + e]
@@ -288,92 +295,152 @@
     def _():
         sin[...] = as_row(whole[:, half:half + 128])
 
-    def mixed_in(j):
-        wait_for(mixed.at[j], mr.at[j])
-
-        @pl.when(l < last)
-        def _():
-            send(mixed.at[j], mixed.at[j], ms.at[j], mr.at[j], above)
-
-    def far(j, carry):
-        mixed_in(j)
+    def add(j):
         wait_second(d2r.at[j])
         acc[...] += dot(mixed[j], g[j].reshape(width, half))
+
+    def take(j):
+        wait_for(mixed.at[j], mr.at[j])
+
+        @pl.when(l < last)
+        def _():
+            send(mixed.at[j], mixed.at[j], ms.at[j], mr.at[j], above)
+
+    def far(j, carry):
+        take(j)
+        send(mixed.at[j], mixed.at[j], mc.at[j], mr.at[j], core_peer)
+        add(j)
         return carry
 
-    lax.fori_loop(0, l - 1, far, 0)
-    p2[c] = acc[...]
-    send(p2.at[c], p2.at[c], ex.at[0], ex.at[1], core_peer)
-    wait_second(d2r.at[l])
-    wait_for(wq.at[:, :, pl.ds(0, half)], qsem.at[5])
-    wait_for(p2.at[1 - c], ex.at[1])
-
-    @pl.when(l == 0)
+    def far_helper(j, carry):
+        wait_for(mixed.at[j], mr.at[j])
+        add(j)
+        return carry
+
+    def pass_down(s, carry):
+        ring_step(s)
+        return carry
+
+    later = jnp.maximum(ready, early)
+
+    @pl.when(c == 1)
     def _():
-        near2[...] = jnp.zeros_like(near2)
-
-    @pl.when(l > 0)
+        lax.fori_loop(0, l - close, far_helper, 0)
+        p2[...] = acc[...]
+        send(p2, p2, ex.at[0], ex.at[1], core_peer)
+        lax.fori_loop(later, up_steps, pass_down, 0)
+        wait_second(d2r.at[l])
+
+    @pl.when(c == 0)
     def _():
-        wait_for(gnear, nx.at[1])
-        mixed_in(l - 1)
-        got = mixed[l - 1]
-        near2[c] = dot(got, g[l - 1].reshape(width, half))
-        near2[1 - c] = dot(got, gnear[...].reshape(width, half))
-
-    part = jnp.concatenate([p2[0] + near2[0], p2[1] + near2[1]], axis=1)
-    scale = lax.rsqrt(jnp.mean(part * part, axis=1, keepdims=True) + 1e-06)
-    latent = (part * scale * gain_ref[...].astype(F32)).astype(BF16)
-    query = dot(latent, wq[...].reshape(width, width)).astype(BF16)
-    logits = nt_dot(query, latent) * (1.0 / float(width) ** 0.5)
-    logits = jnp.where(maskv[...] > 0.5, logits, -1e30)
-    top = jnp.max(logits, axis=1, keepdims=True)
-    raised = jnp.exp(logits - top)
-    weights = (raised / jnp.sum(raised, axis=1, keepdims=True)).astype(BF16)
-    mixed[l] = dot(weights, latent).astype(BF16)
-
-    @pl.when(l < last)
+        lax.fori_loop(0, l - close, far, 0)
+        for k in range(close - 1, 0, -1):
+            @pl.when(l > k)
+            def _():
+                take(l - 1 - k)
+
+        wait_for(wq.at[:, :, pl.ds(0, half)], qsem.at[5])
+        wait_for(p2, ex.at[1])
+        near2[0] = acc[...]
+        near2[1] = p2[...]
+
+        def near(k):
+            wait_for(gnear.at[k], nx.at[close + k])
+            wait_second(d2r.at[l - 1 - k])
+            got = mixed[l - 1 - k]
+            near2[0] += dot(got, g[l - 1 - k].reshape(width, half))
+            near2[1] += dot(got, gnear[k].reshape(width, half))
+
+        for k in range(close - 1, 0, -1):
+            @pl.when(l > k)
+            def _():
+                near(k)
+
+        @pl.when(l > 0)
+        def _():
+            wait_for(mixed.at[l - 1], mr.at[l - 1])
+            near(0)
+
+        part = jnp.concatenate([near2[0], near2[1]], axis=1)
+        scale = lax.rsqrt(jnp.mean(part * part, axis=1, keepdims=True) + 1e-06)
+        latent = (part * scale * gain_ref[...].astype(F32)).astype(BF16)
+        query = dot(latent, wq[...].reshape(width, width)).astype(BF16)
+        logits = nt_dot(query, latent) * (1.0 / float(width) ** 0.5)
+        logits = jnp.where(maskv[...] > 0.5, logits, -1e30)
+        top = jnp.max(logits, axis=1, keepdims=True)
+        raised = jnp.exp(logits - top)
+        weights = (raised / jnp.sum(raised, axis=1, keepdims=True)).astype(BF16)
+        mixed[l] = dot(weights, latent).astype(BF16)
+
+        @pl.when(l < last)
+        def _():
+            send(mixed.at[l], mixed.at[l], ms.at[l], mr.at[l], above)
+
+        latv[...] = latent
+        wait_second(d2r.at[l])
+        value = as_row(dot(mixed[l], g[l].reshape(width, half)[:, 0:128]))
+
+        @pl.when(l < last)
+        def _():
+            wait_for(mixed.at[l], ms.at[l])
+
+        @pl.when(l + 1 < last)
+        def _():
+            send(mixed.at[l], mixed.at[l], ms.at[n], mr.at[l], above_two)
+
+        @pl.when(l > 0)
+        def _():
+            wait_for(sin, ssem.at[1])
+
+        sout[...] = sin[...] + value
+
+        @pl.when(l < last)
+        def _():
+            send(sout, sin, ssem.at[0], ssem.at[1], above)
+
+        @pl.when(l == last)
+        def _():
+            fin[e] = sout[...]
+            send(sout, fin.at[e], fs.at[last], fr.at[e], (l, d, tensor_of(1 - e, 0)))
+
+            def one(p, carry):
+                for k in range(2):
+                    send(
+                        sout, fin.at[e], fs.at[p + k * n], fr.at[e],
+                        (p, d, tensor_of(k, 0)),
+                    )
+                return carry
+            lax.fori_loop(0, last, one, 0)
+
+        @pl.when(e == 0)
+        def _():
+            lat[0] = latent
+            for k in range(1, 4):
+                send(latv, lat.at[0], lats.at[k], latr.at[0], (l, d, k))
+
+        @pl.when(e == 1)
+        def _():
+            for k in range(4):
+                send(latv, lat.at[1], lats.at[k], latr.at[1], mirror[k])
+
+        lax.fori_loop(later, up_steps, pass_down, 0)
+
+        @pl.when(l < last)
+        def _():
+            wait_for(fin.at[0], fr.at[0])
+            wait_for(fin.at[1], fr.at[1])
+
+        @pl.when(l == last)
+        def _():
+            wait_for(fin.at[1 - e], fr.at[1 - e])
+
+        send(fin, fin, fs.at[2 * n - 1], fr.at[2], core_peer)
+
+    @pl.when(c == 1)
     def _():
-        send(mixed.at[l], mixed.at[l], ms.at[l], mr.at[l], above)
-
-    latv[...] = latent
-
-    @pl.when(e == 0)
-    def _():
-        lat[0] = latent
-        send(latv, lat.at[0], lats.at[0], latr.at[0], (l, d, tensor_of(1, c)))
-
-    @pl.when(e == 1)
-    def _():
-        for k in range(2):
-            send(latv, lat.at[1], lats.at[k], latr.at[1], mirror[k])
-
-    value = as_row(dot(mixed[l], g[l].reshape(width, half)[:, 0:128]))
-
-    @pl.when(l > 0)
-    def _():
-        wait_for(sin, ssem.at[1])
-
-    sout[...] = sin[...] + value
-
-    @pl.when(l < last)
-    def _():
-        send(sout, sin, ssem.at[0], ssem.at[1], above)
-        wait_for(fin.at[0], fr.at[0])
-        wait_for(fin.at[1], fr.at[1])
-
-    @pl.when(l == last)
-    def _():
-        fin[e] = sout[...]
-        send(sout, fin.at[e], fs.at[last], fr.at[e], (l, d, tensor_of(1 - e, c)))
-
-        def one(p, carry):
-            for k in range(2):
-                send(sout, fin.at[e], fs.at[p + k * n], fr.at[e], (p, d, tensor_of(k, c)))
-            return carry
-        lax.fori_loop(0, last, one, 0)
-        wait_for(fin.at[1 - e], fr.at[1 - e])
-
-    @pl.when(e == 1)
+        wait_for(fin, fr.at[2])
+
+    @pl.when(t > 0)
     def _():
         wait_for(lat.at[0], latr.at[0])
 
@@ -382,12 +449,13 @@
     score_out[0:1, :] = fin[0, 0:1, 0:seq]
     score_out[1:2, :] = fin[1, 0:1, 0:seq]
 
-    wait_for(wd.at[pl.ds(0, (nd - 1) * rows)], asem.at[0])
+    wait_for(wd.at[own_rows], asem.at[0])
+    if ny > 1:
+        wait_for(y_bytes, asem.at[2])
+        wait_for(y_bytes, asem.at[4])
     wait_first(qsem.at[0])
     wait_second(qsem.at[2])
-    wait_for(wq.at[:, :, pl.ds(0, half)], qsem.at[4])
     wait_for(p0recv.at[pl.ds(0, 3)], psem.at[0])
-    wait_for(p2.at[c], ex.at[0])
 
     def ring_left(s, carry):
         @pl.when((s <= l) & (l < last))
@@ -406,36 +474,54 @@
         wait_first(d1s.at[j])
         wait_second(d2s.at[j])
 
+        @pl.when((l < last) & (j < l - 1) & (c == 0))
+        def _():
+            wait_for(mixed.at[j], ms.at[j])
+
+        @pl.when((j < l - close) & (c == 0))
+        def _():
+            wait_for(mixed.at[j], mc.at[j])
+        return carry
+
+    lax.fori_loop(0, l + 1, item_left, 0)
+
+    @pl.when(c == 1)
+    def _():
+        wait_for(wq.at[:, :, pl.ds(0, half)], qsem.at[4])
+        wait_for(p2, ex.at[0])
+        for k in range(close):
+            @pl.when(l > k)
+            def _():
+                wait_for(gnear.at[k], nx.at[k])
+
+    @pl.when(c == 0)
+    def _():
+        @pl.when(l + 1 < last)
+        def _():
+            wait_for(mixed.at[l], ms.at[n])
+
+        for k in range(1, 4):
+            wait_for(latv, lats.at[k])
+
+        @pl.when(e == 1)
+        def _():
+            wait_for(latv, lats.at[0])
+
         @pl.when(l < last)
         def _():
-            wait_for(mixed.at[j], ms.at[j])
-        return carry
-
-    lax.fori_loop(0, l + 1, item_left, 0)
-
-    @pl.when(l > 0)
-    def _():
-        wait_for(gnear, nx.at[0])
-
-    wait_for(latv, lats.at[0])
-
-    @pl.when(e == 1)
-    def _():
-        wait_for(latv, lats.at[1])
-
-    @pl.when(l < last)
-    def _():
-        wait_for(sout, ssem.at[0])
-
-    @pl.when(l == last)
-    def _():
-        wait_for(sout, fs.at[last])
-
-        def one(p, carry):
-            wait_for(sout, fs.at[p])
-            wait_for(sout, fs.at[p + n])
-            return carry
-        lax.fori_loop(0, last, one, 0)
+            wait_for(sout, ssem.at[0])
+
+        wait_for(fin, fs.at[2 * n - 1])
+
+        @pl.when(l == last)
+        def _():
+            wait_for(sout, fs.at[last])
+
+            def one(p, carry):
+                wait_for(sout, fs.at[p])
+                wait_for(sout, fs.at[p + n])
+                return carry
+            lax.fori_loop(0, last, one, 0)
 
 
 def body(inputs, lengths, w_down, w_query, w_out, gain_latent, readout):
@@ -466,11 +552,11 @@
             pltpu.VMEM((n, 4, rows, quarter), BF16),
             pltpu.VMEM((n, 4, rows, quarter), BF16),
             pltpu.VMEM((n, nd // 2, 2 * rows, half), BF16),
-            pltpu.VMEM((nd // 2, 2 * rows, half), BF16),
+            pltpu.VMEM((3, nd // 2, 2 * rows, half), BF16),
             pltpu.VMEM((4, seq, half + 128), F32),
             pltpu.VMEM((4, seq, half + 128), F32),
             pltpu.VMEM((seq, half), F32),
-            pltpu.VMEM((2, seq, half), F32),
+            pltpu.VMEM((seq, half), F32),
             pltpu.VMEM((2, seq, half), F32),
             pltpu.VMEM((n, seq, width), BF16),
             pltpu.VMEM((seq, width), BF16),
@@ -479,9 +565,9 @@
             pltpu.VMEM((8, 128), F32),
             pltpu.VMEM((2, 8, 128), F32),
             pltpu.VMEM((seq, seq), F32),
-            pltpu.VMEM((3 * max(nd // 2, 1), rows, quarter), BF16),
+            pltpu.VMEM((max(4 * (nd // 2 - 1), 3), rows, quarter), BF16),
             dma((4,)),
-            dma((2,)),
+            dma((6,)),
             dma((6,)),
             dma((up_steps,)),
             dma((up_steps,)),
@@ -493,16 +579,17 @@
             dma((n,)),
             dma((n,)),
             dma((n,)),
+            dma((6,)),
+            dma((2,)),
+            dma((n + 1,)),
+            dma((n,)),
+            dma((n,)),
             dma((2,)),
             dma((2,)),
-            dma((n,)),
-            dma((n,)),
-            dma((2,)),
-            dma((2,)),
-            dma((2,)),
+            dma((4,)),
             dma((2,)),
             dma((2 * n,)),
-            dma((2,)),
+            dma((3,)),
         ],
         compiler_params=pltpu.CompilerParams(
             collective_id=0, has_side_effects=True, vmem_limit_bytes=40 * 1024 * 1024

time: 174 us -> 148 us (0.85)
  Pallas kernels: 167 us -> 142 us
    pallas_call x1, Pallas kernels: 167 us -> 142 us  [body(): pl.pallas_call(functools.partial(kernel, n, nd), out_shape=(jax.ShapeDtyp...]
where the time goes in v2:
time: 148 us; the launch traced here: 147 us
  Pallas kernels  142 us (96%)
  local copies, waits for them, and re-layouts  4.83 us (3%)
    pallas_call x1, Pallas kernels, body(): pl.pallas_call(functools.partial(kernel, n, nd), out_shape=(jax.ShapeDtyp...  142 us
    unnamed x14, local copies, waits for them, and re-layouts  4.12 us

profile of v2, /device:TPU:1, one launch (start us, length us, event | category | flops | bytes accessed | tf_op | source)
XLA Modules:
  0.0 147.3 jit_solution(12336619283316421594)
XLA Ops:
  0.6 0.0 copy-start.3
  0.6 0.0 copy-start.4
  0.7 0.0 copy-start.5
  0.7 0.7 reshape.21.read_ref
  1.4 0.0 copy-done.3
  1.4 0.0 copy-done.4
  1.4 0.0 copy-done.5
  1.4 0.0 copy-start
  1.4 1.0 copy-done
  2.4 0.0 copy-start.1
  2.4 0.9 copy-done.1
  3.4 0.0 copy-start.2
  3.4 0.9 copy-done.2
  4.3 141.8 %shard_map.86 = (bf16[2,64,512]{2,1,0:T(8,128)(2,1)S(1)}, f32[2,64]{1,0:T(2,128)S(1)}) custom-call(bf16[128,1792]{1,0:T(8,128)(2,1)S(1)} %bitcast.13, s32[2,4]{1,0:T(2,128)S(1)} %bitcast.18, bf16[64,1792]{1,0:T(8,128)(2,1)S(1)} %bitcast.14, bf16[64,128]{1,0:T(8,128)(2,1)S(1)} %bitcast.17, bf16[64,1792]{1,0:T(8,128)(2,1)S(1)} %bitcast.15, ...), custom_call_target="tpu_custom_call" | custom-call | tf_op jit(solution)/shard_map/pallas_call | solution.py:539
  146.1 0.7 copy.13
  146.7 0.6 copy.14
Async XLA Ops:
  0.6 0.7 copy-start.3
  0.6 0.7 copy-start.4
  0.7 0.7 copy-start.5
  1.4 1.0 copy-start
  2.4 0.9 copy-start.1
  3.4 0.9 copy-start.2

commit v3 on v2

--- a/solution.py
+++ b/solution.py
@@ -60,7 +60,7 @@
     below = ((l + n - 1) % n, d, t)
     above_two = ((l + 2) % n, d, t)
     below_two = ((l + n - 2) % n, d, t)
-    mirror = [(last - l, d, k) for k in range(4)]
+    mirror = (last - l, d, t)
 
     def send(src, dst, ssem_, rsem_, device):
         pltpu.make_async_remote_copy(
@@ -91,132 +91,18 @@
         pl.semaphore_signal(barrier, inc=1, device_id=device, device_id_type=MESH)
 
     greeted = x_peers + y_peers + [core_peer, (l, d, tensor_of(1 - e, 1 - c))]
-    greeted += [above, below, above_two, below_two]
+    greeted += [above, below, above_two, below_two, mirror]
     for device in greeted:
         greet(device)
 
-    greet((last - l, d, tensor_of(1, 0)))
-    pl.semaphore_wait(barrier, len(greeted) + jnp.where(t == tensor_of(1, 0), 4, 0))
-
     for copy in local:
         copy.wait()
-
-    far_rows = pl.ds(pl.multiple_of((2 * y + 1 - xh) * rows, rows), rows)
-    y_bytes = wd.at[pl.ds(0, (ny - 1) * rows)]
-
-    def gather_y(cols, s_sem, r_sem):
-        for device in y_peers:
-            send(wd.at[cols], wd.at[cols], s_sem, r_sem, device)
-
-    send(wd.at[own_rows], wd.at[own_rows], asem.at[0], asem.at[1], x_peers[0])
-    gather_y(own_rows, asem.at[2], asem.at[3])
-
-    def up_send(s):
-        @pl.when((s <= l) & (l < last) & (s < up_steps))
-        def _():
-            j = l - s
-            send(ring.at[j], ring.at[j], ups.at[s], upr.at[s], above)
-
-    def down_valid(who, s):
-        return (s < up_steps - 1) & ((who + s <= low) | (who + s >= n))
-
-    def down_send(s):
-        @pl.when(down_valid(l, s))
-        def _():
-            j = (l + s) % n
-            send(ring.at[j], ring.at[j], dns.at[s], dnr.at[s], below)
-
-    behind = (l + 1) % n
-
-    def ring_step(s):
-        @pl.when(s < l)
-        def _():
-            wait_for(ring.at[l - 1 - s], upr.at[s])
-            up_send_next(s)
-
-        @pl.when(down_valid(behind, s))
-        def _():
-            wait_for(ring.at[(l + 1 + s) % n], dnr.at[s])
-            down_send_next(s)
-
-    def up_send_next(s):
-        @pl.when(s + 1 < up_steps)
-        def _():
-            up_send(s + 1)
-
-    def down_send_next(s):
-        @pl.when(s + 1 < up_steps - 1)
-        def _():
-            down_send(s + 1)
-
-    up_send(0)
-    down_send(0)
-
-    def spread_first(ref, cols, s_sem, r_sem):
-        for device in x_peers:
-            piece = ref.at[y, pair_rows, cols]
-            send(piece, piece, s_sem, r_sem, device)
-
-    def wait_first(sem):
-        wait_for(dummy.at[pl.ds(0, 3)], sem)
-
-    def spread_second(piece, s_sem, r_sem):
-        for device in y_peers:
-            send(piece, piece, s_sem, r_sem, device)
-
-    def wait_second(sem):
-        if ny > 1:
-            wait_for(dummy, sem)
-
-    spread_first(wq, query_cols, qsem.at[0], qsem.at[1])
-
-    def cut_send(j, part):
-        for b in range(4):
-            csend[j, b] = part[:, b * quarter:(b + 1) * quarter].astype(BF16)
-        for x_low, core in cut_peers:
-            send(
-                csend.at[j, 2 * core + x_low], crecv.at[j, t], cs.at[j], cr.at[j],
-                (l, d, tensor_of(x_low, core)),
-            )
-
-    def cut_sum(j):
-        wait_for(dummy.at[pl.ds(0, 3)], cr.at[j])
-        crecv[j, t] = csend[j, 2 * c + e]
-        total = crecv[j, 0].astype(F32)
-        for k in range(1, 4):
-            total = total + crecv[j, k].astype(F32)
-        g[j, y, pair_rows, own_cols] = total.astype(BF16)
-        spread_first(g.at[j], own_cols, d1s.at[j], d1r.at[j])
-
-    def pass_on(j):
-        wait_first(d1r.at[j])
-        spread_second(g.at[j, y], d2s.at[j], d2r.at[j])
-
     seen = jnp.sum(ring[l].astype(F32) * read_ref[...].astype(F32), axis=1, keepdims=True)
-    cut_send(l, jnp.broadcast_to(seen, (rows, width)))
-
-    early = min(3, up_steps)
-    for s in range(early):
-        ring_step(s)
-        if s == 0:
-            cut_sum(l)
-            wait_first(qsem.at[1])
-            for k in range(2):
-                cols = pl.ds(pl.multiple_of((2 * k + c) * quarter, quarter), quarter)
-                spread_second(wq.at[y, :, cols], qsem.at[2], qsem.at[3])
-            wait_for(wd.at[far_rows], asem.at[1])
-            gather_y(far_rows, asem.at[4], asem.at[5])
-        if s == 1:
-            pass_on(l)
-            wait_second(qsem.at[3])
-
-            @pl.when(c == 1)
-            def _():
-                for k in range(2):
-                    cols = pl.ds((2 * k + 1) * quarter, quarter)
-                    piece = wq.at[:, :, cols]
-                    send(piece, piece, qsem.at[4], qsem.at[5], core_peer)
-
+    head = jnp.sum(xv[...].astype(F32) * read_ref[...].astype(F32), axis=1, keepdims=True)
+    for b in range(4):
+        p0send[b, :, half:half + 128] = jnp.broadcast_to(
+            head[(b % 2) * seq:(b % 2 + 1) * seq], (seq, 128)
+        ).astype(BF16)
     i0 = lax.broadcasted_iota(jnp.int32, (seq, seq), 0)
     i1 = lax.broadcasted_iota(jnp.int32, (seq, seq), 1)
     doc0 = jnp.zeros((seq, seq), jnp.int32)
@@ -228,18 +114,131 @@
         doc1 = doc1 + (i1 >= end).astype(jnp.int32)
     maskv[...] = ((doc0 == doc1) & (i1 <= i0)).astype(F32)
 
+    pl.semaphore_wait(barrier, len(greeted))
+
+    far_rows = pl.ds(pl.multiple_of((2 * y + 1 - xh) * rows, rows), rows)
+    y_bytes = wd.at[pl.ds(0, (ny - 1) * rows)]
+
+    def gather_y(cols, s_sem, r_sem):
+        for device in y_peers:
+            send(wd.at[cols], wd.at[cols], s_sem, r_sem, device)
+
+    send(wd.at[own_rows], wd.at[own_rows], asem.at[0], asem.at[1], x_peers[0])
+    gather_y(own_rows, asem.at[2], asem.at[3])
+
+    def up_send(s):
+        @pl.when((s <= l) & (l < last) & (s < up_steps))
+        def _():
+            j = l - s
+            send(ring.at[j], ring.at[j], ups.at[s], upr.at[s], above)
+
+    def down_valid(who, s):
+        return (s < up_steps - 1) & ((who + s <= low) | (who + s >= n))
+
+    def down_send(s):
+        @pl.when(down_valid(l, s))
+        def _():
+            j = (l + s) % n
+            send(ring.at[j], ring.at[j], dns.at[s], dnr.at[s], below)
+
+    behind = (l + 1) % n
+
+    def ring_step(s):
+        @pl.when(s < l)
+        def _():
+            wait_for(ring.at[l - 1 - s], upr.at[s])
+            up_send_next(s)
+
+        @pl.when(down_valid(behind, s))
+        def _():
+            wait_for(ring.at[(l + 1 + s) % n], dnr.at[s])
+            down_send_next(s)
+
+    def up_send_next(s):
+        @pl.when(s + 1 < up_steps)
+        def _():
+            up_send(s + 1)
+
+    def down_send_next(s):
+        @pl.when(s + 1 < up_steps - 1)
+        def _():
+            down_send(s + 1)
+
+    up_send(0)
+    down_send(0)
+
+    def spread_first(ref, cols, s_sem, r_sem):
+        for device in x_peers:
+            piece = ref.at[y, pair_rows, cols]
+            send(piece, piece, s_sem, r_sem, device)
+
+    def wait_first(sem):
+        wait_for(dummy.at[pl.ds(0, 3)], sem)
+
+    def spread_second(piece, s_sem, r_sem):
+        for device in y_peers:
+            send(piece, piece, s_sem, r_sem, device)
+
+    def wait_second(sem):
+        if ny > 1:
+            wait_for(dummy, sem)
+
+    spread_first(wq, query_cols, qsem.at[0], qsem.at[1])
+
+    def cut_send(j, part):
+        for b in range(4):
+            csend[j, b] = part[:, b * quarter:(b + 1) * quarter].astype(BF16)
+        for x_low, core in cut_peers:
+            send(
+                csend.at[j, 2 * core + x_low], crecv.at[j, t], cs.at[j], cr.at[j],
+                (l, d, tensor_of(x_low, core)),
+            )
+
+    def cut_sum(j):
+        wait_for(dummy.at[pl.ds(0, 3)], cr.at[j])
+        crecv[j, t] = csend[j, 2 * c + e]
+        total = crecv[j, 0].astype(F32)
+        for k in range(1, 4):
+            total = total + crecv[j, k].astype(F32)
+        g[j, y, pair_rows, own_cols] = total.astype(BF16)
+        spread_first(g.at[j], own_cols, d1s.at[j], d1r.at[j])
+
+    def pass_on(j):
+        wait_first(d1r.at[j])
+        spread_second(g.at[j, y], d2s.at[j], d2r.at[j])
+
+    cut_send(l, jnp.broadcast_to(seen, (rows, width)))
+
+    early = min(3, up_steps)
+    for s in range(early):
+        ring_step(s)
+        if s == 0:
+            wait_for(wd.at[far_rows], asem.at[1])
+            gather_y(far_rows, asem.at[4], asem.at[5])
+            cut_sum(l)
+            wait_first(qsem.at[1])
+            for k in range(2):
+                cols = pl.ds(pl.multiple_of((2 * k + c) * quarter, quarter), quarter)
+                spread_second(wq.at[y, :, cols], qsem.at[2], qsem.at[3])
+        if s == 1:
+            pass_on(l)
+            wait_second(qsem.at[3])
+
+            @pl.when(c == 1)
+            def _():
+                for k in range(2):
+                    cols = pl.ds((2 * k + 1) * quarter, quarter)
+                    piece = wq.at[:, :, cols]
+                    send(piece, piece, qsem.at[4], qsem.at[5], core_peer)
+
     if ny > 1:
         wait_for(y_bytes, asem.at[3])
         wait_for(y_bytes, asem.at[5])
-    head = jnp.sum(xv[...].astype(F32) * read_ref[...].astype(F32), axis=1, keepdims=True)
     for core in range(2):
         part = nt_dot(xv[...], wd[core * half:(core + 1) * half])
         for x_low in range(2):
             b = 2 * core + x_low
-            p0send[b, :, 0:half] = part[x_low * seq:(x_low + 1) * seq]
-            p0send[b, :, half:half + 128] = jnp.broadcast_to(
-                head[x_low * seq:(x_low + 1) * seq], (seq, 128)
-            )
+            p0send[b, :, 0:half] = part[x_low * seq:(x_low + 1) * seq].astype(BF16)
     for x_low, core in cut_peers:
         send(
             p0send.at[2 * core + x_low], p0recv.at[t], psem.at[0], psem.at[1],
@@ -279,9 +278,9 @@
 
     wait_for(p0recv.at[pl.ds(0, 3)], psem.at[1])
     p0recv[t] = p0send[2 * c + e]
-    whole = p0recv[0]
+    whole = p0recv[0].astype(F32)
     for k in range(1, 4):
-        whole = whole + p0recv[k]
+        whole = whole + p0recv[k].astype(F32)
     acc[...] = whole[:, 0:half]
     s0 = lax.broadcasted_iota(jnp.int32, (seq, 128), 0)
     s1 = lax.broadcasted_iota(jnp.int32, (seq, 128), 1)
@@ -323,6 +322,14 @@
 
     later = jnp.maximum(ready, early)
 
+    def spread_scores(core, x_low):
+        def one(i, carry):
+            step = (i + 1) // 2
+            p = last - up_steps + jnp.where(i % 2 == 0, step, -step)
+            send(fin.at[e], fin.at[e], fs.at[p], fr.at[e], (p, d, tensor_of(x_low, core)))
+            return carry
+        lax.fori_loop(0, last, one, 0)
+
     @pl.when(c == 1)
     def _():
         lax.fori_loop(0, l - close, far_helper, 0)
@@ -330,6 +337,14 @@
         send(p2, p2, ex.at[0], ex.at[1], core_peer)
         lax.fori_loop(later, up_steps, pass_down, 0)
         wait_second(d2r.at[l])
+
+        @pl.when(l == last)
+        def _():
+            wait_for(fin.at[e], fr.at[e])
+            send(
+                fin.at[e], fin.at[e], fs.at[last], fr.at[e], (l, d, tensor_of(1 - e, 1))
+            )
+            spread_scores(1, 1 - e)
 
     @pl.when(c == 0)
     def _():
@@ -364,6 +379,23 @@
         part = jnp.concatenate([near2[0], near2[1]], axis=1)
         scale = lax.rsqrt(jnp.mean(part * part, axis=1, keepdims=True) + 1e-06)
         latent = (part * scale * gain_ref[...].astype(F32)).astype(BF16)
+        latv[...] = latent
+
+        def keep():
+            @pl.when(e == 0)
+            def _():
+                lat[0] = latv[...]
+                for k in range(1, 4):
+                    send(latv, lat.at[0], lats.at[k], latr.at[0], (l, d, k))
+
+            @pl.when(e == 1)
+            def _():
+                send(latv, lat.at[1], lats.at[0], latr.at[1], mirror)
+
+        @pl.when(l == last)
+        def _():
+            keep()
+
         query = dot(latent, wq[...].reshape(width, width)).astype(BF16)
         logits = nt_dot(query, latent) * (1.0 / float(width) ** 0.5)
         logits = jnp.where(maskv[...] > 0.5, logits, -1e30)
@@ -376,10 +408,19 @@
         def _():
             send(mixed.at[l], mixed.at[l], ms.at[l], mr.at[l], above)
 
-        latv[...] = latent
         wait_second(d2r.at[l])
         value = as_row(dot(mixed[l], g[l].reshape(width, half)[:, 0:128]))
 
+        @pl.when(l > 0)
+        def _():
+            wait_for(sin, ssem.at[1])
+
+        sout[...] = sin[...] + value
+
+        @pl.when(l < last)
+        def _():
+            send(sout, sin, ssem.at[0], ssem.at[1], above)
+
         @pl.when(l < last)
         def _():
             wait_for(mixed.at[l], ms.at[l])
@@ -388,66 +429,23 @@
         def _():
             send(mixed.at[l], mixed.at[l], ms.at[n], mr.at[l], above_two)
 
-        @pl.when(l > 0)
-        def _():
-            wait_for(sin, ssem.at[1])
-
-        sout[...] = sin[...] + value
-
-        @pl.when(l < last)
-        def _():
-            send(sout, sin, ssem.at[0], ssem.at[1], above)
-
         @pl.when(l == last)
         def _():
             fin[e] = sout[...]
-            send(sout, fin.at[e], fs.at[last], fr.at[e], (l, d, tensor_of(1 - e, 0)))
-
-            def one(p, carry):
-                for k in range(2):
-                    send(
-                        sout, fin.at[e], fs.at[p + k * n], fr.at[e],
-                        (p, d, tensor_of(k, 0)),
-                    )
-                return carry
-            lax.fori_loop(0, last, one, 0)
-
-        @pl.when(e == 0)
-        def _():
-            lat[0] = latent
-            for k in range(1, 4):
-                send(latv, lat.at[0], lats.at[k], latr.at[0], (l, d, k))
-
-        @pl.when(e == 1)
-        def _():
-            for k in range(4):
-                send(latv, lat.at[1], lats.at[k], latr.at[1], mirror[k])
+            send(fin.at[e], fin.at[e], fs.at[2 * n - 1], fr.at[e], core_peer)
+            spread_scores(0, e)
+
+        @pl.when(l < last)
+        def _():
+            keep()
 
         lax.fori_loop(later, up_steps, pass_down, 0)
 
-        @pl.when(l < last)
-        def _():
-            wait_for(fin.at[0], fr.at[0])
-            wait_for(fin.at[1], fr.at[1])
-
-        @pl.when(l == last)
-        def _():
-            wait_for(fin.at[1 - e], fr.at[1 - e])
-
-        send(fin, fin, fs.at[2 * n - 1], fr.at[2], core_peer)
-
-    @pl.when(c == 1)
-    def _():
-        wait_for(fin, fr.at[2])
-
-    @pl.when(t > 0)
-    def _():
-        wait_for(lat.at[0], latr.at[0])
-
-    wait_for(lat.at[1], latr.at[1])
-    lat_out[...] = lat[...]
-    score_out[0:1, :] = fin[0, 0:1, 0:seq]
-    score_out[1:2, :] = fin[1, 0:1, 0:seq]
+    @pl.when(t == tensor_of(1, 0))
+    def _():
+        wait_for(lat.at[1], latr.at[1])
+        for i, k in enumerate((0, 1, 3)):
+            send(lat.at[1], lat.at[1], lats.at[1 + i], latr.at[1], (l, d, k))
 
     wait_for(wd.at[own_rows], asem.at[0])
     if ny > 1:
@@ -511,17 +509,45 @@
         def _():
             wait_for(sout, ssem.at[0])
 
-        wait_for(fin, fs.at[2 * n - 1])
-
-        @pl.when(l == last)
-        def _():
-            wait_for(sout, fs.at[last])
-
-            def one(p, carry):
-                wait_for(sout, fs.at[p])
-                wait_for(sout, fs.at[p + n])
-                return carry
-            lax.fori_loop(0, last, one, 0)
+    @pl.when(t > 0)
+    def _():
+        wait_for(lat.at[0], latr.at[0])
+
+    @pl.when(t != tensor_of(1, 0))
+    def _():
+        wait_for(lat.at[1], latr.at[1])
+
+    lat_out[...] = lat[...]
+
+    @pl.when(c == 0)
+    def _():
+        @pl.when(l < last)
+        def _():
+            wait_for(fin.at[e], fr.at[e])
+            send(fin.at[e], fin.at[e], fs.at[2 * n - 1], fr.at[e], core_peer)
+
+        wait_for(fin.at[1 - e], fr.at[1 - e])
+
+    @pl.when(c == 1)
+    def _():
+        wait_for(fin.at[1 - e], fr.at[1 - e])
+        send(fin.at[1 - e], fin.at[1 - e], fs.at[2 * n - 1], fr.at[1 - e], core_peer)
+
+        @pl.when(l < last)
+        def _():
+            wait_for(fin.at[e], fr.at[e])
+
+    score_out[0:1, :] = fin[0, 0:1, 0:seq]
+    score_out[1:2, :] = fin[1, 0:1, 0:seq]
+
+    wait_for(fin.at[0], fs.at[2 * n - 1])
+
+    @pl.when(l == last)
+    def _():
+        def one(p, carry):
+            wait_for(fin.at[0], fs.at[p])
+            return carry
+        lax.fori_loop(0, last + c, one, 0)
 
 
 def body(inputs, lengths, w_down, w_query, w_out, gain_latent, readout):
@@ -553,8 +579,8 @@
             pltpu.VMEM((n, 4, rows, quarter), BF16),
             pltpu.VMEM((n, nd // 2, 2 * rows, half), BF16),
             pltpu.VMEM((3, nd // 2, 2 * rows, half), BF16),
-            pltpu.VMEM((4, seq, half + 128), F32),
-            pltpu.VMEM((4, seq, half + 128), F32),
+            pltpu.VMEM((4, seq, half + 128), BF16),
+            pltpu.VMEM((4, seq, half + 128), BF16),
             pltpu.VMEM((seq, half), F32),
             pltpu.VMEM((seq, half), F32),
             pltpu.VMEM((2, seq, half), F32),
@@ -592,7 +618,7 @@
             dma((3,)),
         ],
         compiler_params=pltpu.CompilerParams(
-            collective_id=0, has_side_effects=True, vmem_limit_bytes=40 * 1024 * 1024
+            collective_id=0, has_side_effects=True, vmem_limit_bytes=60 * 1024 * 1024
         ),
     )(
         inputs.reshape(2 * seq, feats),

time: 148 us -> 141 us (0.953)
  Pallas kernels: 142 us -> 137 us
    pallas_call x1, Pallas kernels: 142 us -> 137 us  [body(): pl.pallas_call(functools.partial(kernel, n, nd), out_shape=(jax.ShapeDtyp...]
    unnamed x14 -> x6, local copies, waits for them, and re-layouts: 4.12 us -> 2.81 us
where the time goes in v3:
time: 141 us
  Pallas kernels  137 us (97%)
  local copies, waits for them, and re-layouts  3.41 us (2%)
    pallas_call x1, Pallas kernels, body(): pl.pallas_call(functools.partial(kernel, n, nd), out_shape=(jax.ShapeDtyp...  137 us

profile of v3, /device:TPU:1, one launch (start us, length us, event | category | flops | bytes accessed | tf_op | source)
XLA Modules:
  0.0 141.1 jit_solution(17108712179775815238)
XLA Ops:
  0.6 0.0 copy-start
  0.6 0.7 copy-done
  1.3 0.6 reshape.21.read_ref
  1.9 137.0 %shard_map.86 = (bf16[2,64,512]{2,1,0:T(8,128)(2,1)}, f32[2,64]{1,0:T(2,128)}) custom-call(bf16[128,1792]{1,0:T(8,128)(2,1)} %bitcast.13, s32[2,4]{1,0:T(2,128)} %bitcast.18, bf16[64,1792]{1,0:T(8,128)(2,1)} %bitcast.14, bf16[64,128]{1,0:T(8,128)(2,1)} %bitcast.17, bf16[64,1792]{1,0:T(8,128)(2,1)} %bitcast.15, bf16[1,512]{1,0:T(2,128)(2,1)} %gain_ref.1, ...), custom_call_target="tpu_custom_call" | custom-call | tf_op jit(solution)/shard_map/pallas_call | solution.py:565
  138.9 0.0 copy-start.1
  138.9 1.6 %copy.13 = bf16[1,2,1,64,512]{4,3,2,1,0:T(8,128)(2,1)} copy(bf16[1,2,1,64,512]{4,3,2,1,0:T(8,128)(2,1)} %bitcast.16) | data formatting | bytes 262144
  140.5 0.0 copy-done.1
  140.5 0.6 copy.14
Async XLA Ops:
  0.6 0.7 copy-start
  138.9 1.6 %copy-start.1 = (f32[2,64]{1,0:T(2,128)S(1)}, f32[2,64]{1,0:T(2,128)}, u32[]{:S(2)}) copy-start(f32[2,64]{1,0:T(2,128)} %get-tuple-element.5) | copy-start | bytes 1540

commit v4 on v3

--- a/solution.py
+++ b/solution.py
@@ -117,14 +117,20 @@
     pl.semaphore_wait(barrier, len(greeted))
 
     far_rows = pl.ds(pl.multiple_of((2 * y + 1 - xh) * rows, rows), rows)
-    y_bytes = wd.at[pl.ds(0, (ny - 1) * rows)]
-
-    def gather_y(cols, s_sem, r_sem):
-        for device in y_peers:
+    facing = ((y + ny // 2) % ny) * 2
+    own_facing = pl.ds(pl.multiple_of((facing + xh) * rows, rows), rows)
+    far_facing = pl.ds(pl.multiple_of((facing + 1 - xh) * rows, rows), rows)
+    y_near = [p for k, p in enumerate(y_peers) if k + 1 != ny // 2]
+    y_facing = [p for k, p in enumerate(y_peers) if k + 1 == ny // 2]
+    near_bytes = wd.at[pl.ds(0, len(y_near) * rows)]
+
+    def shard(cols, s_sem, r_sem, devices):
+        for device in devices:
             send(wd.at[cols], wd.at[cols], s_sem, r_sem, device)
 
-    send(wd.at[own_rows], wd.at[own_rows], asem.at[0], asem.at[1], x_peers[0])
-    gather_y(own_rows, asem.at[2], asem.at[3])
+    shard(own_rows, asem.at[6], asem.at[7], y_facing)
+    shard(own_rows, asem.at[0], asem.at[1], x_peers[:1])
+    shard(own_rows, asem.at[2], asem.at[3], y_near)
 
     def up_send(s):
         @pl.when((s <= l) & (l < last) & (s < up_steps))
@@ -213,15 +219,17 @@
     for s in range(early):
         ring_step(s)
         if s == 0:
+            if y_facing:
+                wait_for(wd.at[own_facing], asem.at[7])
+                shard(own_facing, asem.at[8], asem.at[9], x_peers[:1])
             wait_for(wd.at[far_rows], asem.at[1])
-            gather_y(far_rows, asem.at[4], asem.at[5])
+            shard(far_rows, asem.at[4], asem.at[5], y_near)
             cut_sum(l)
             wait_first(qsem.at[1])
             for k in range(2):
                 cols = pl.ds(pl.multiple_of((2 * k + c) * quarter, quarter), quarter)
                 spread_second(wq.at[y, :, cols], qsem.at[2], qsem.at[3])
         if s == 1:
-            pass_on(l)
             wait_second(qsem.at[3])
 
             @pl.when(c == 1)
@@ -231,9 +239,11 @@
                     piece = wq.at[:, :, cols]
                     send(piece, piece, qsem.at[4], qsem.at[5], core_peer)
 
-    if ny > 1:
-        wait_for(y_bytes, asem.at[3])
-        wait_for(y_bytes, asem.at[5])
+    if y_facing:
+        wait_for(wd.at[far_facing], asem.at[9])
+    if y_near:
+        wait_for(near_bytes, asem.at[3])
+        wait_for(near_bytes, asem.at[5])
     for core in range(2):
         part = nt_dot(xv[...], wd[core * half:(core + 1) * half])
         for x_low in range(2):
@@ -245,6 +255,8 @@
             (l, d, tensor_of(x_low, core)),
         )
 
+    pass_on(l)
+
     def items(s, do):
         @pl.when((s >= 0) & (s < up_steps) & (s < l))
         def _():
@@ -448,9 +460,12 @@
             send(lat.at[1], lat.at[1], lats.at[1 + i], latr.at[1], (l, d, k))
 
     wait_for(wd.at[own_rows], asem.at[0])
-    if ny > 1:
-        wait_for(y_bytes, asem.at[2])
-        wait_for(y_bytes, asem.at[4])
+    if y_facing:
+        wait_for(wd.at[own_rows], asem.at[6])
+        wait_for(wd.at[own_facing], asem.at[8])
+    if y_near:
+        wait_for(near_bytes, asem.at[2])
+        wait_for(near_bytes, asem.at[4])
     wait_first(qsem.at[0])
     wait_second(qsem.at[2])
     wait_for(p0recv.at[pl.ds(0, 3)], psem.at[0])
@@ -593,7 +608,7 @@
             pltpu.VMEM((seq, seq), F32),
             pltpu.VMEM((max(4 * (nd // 2 - 1), 3), rows, quarter), BF16),
             dma((4,)),
-            dma((6,)),
+            dma((10,)),
             dma((6,)),
             dma((up_steps,)),
             dma((up_steps,)),

time: 141 us -> 135 us (0.957)
  Pallas kernels: 137 us -> 131 us
    pallas_call x1, Pallas kernels: 137 us -> 131 us  [body(): pl.pallas_call(functools.partial(kernel, n, nd), out_shape=(jax.ShapeDtyp...]
where the time goes in v4:
time: 135 us
  Pallas kernels  131 us (97%)
  local copies, waits for them, and re-layouts  3.41 us (3%)
    pallas_call x1, Pallas kernels, body(): pl.pallas_call(functools.partial(kernel, n, nd), out_shape=(jax.ShapeDtyp...  131 us
    unnamed x6, local copies, waits for them, and re-layouts  2.81 us

profile of v4, /device:TPU:1, one launch (start us, length us, event | category | flops | bytes accessed | tf_op | source)
XLA Modules:
  0.0 135.2 jit_solution(10594335709107439873)
XLA Ops:
  0.6 0.0 copy-start
  0.6 0.7 copy-done
  1.3 0.6 reshape.21.read_ref
  1.9 131.2 %shard_map.86 = (bf16[2,64,512]{2,1,0:T(8,128)(2,1)}, f32[2,64]{1,0:T(2,128)}) custom-call(bf16[128,1792]{1,0:T(8,128)(2,1)} %bitcast.13, s32[2,4]{1,0:T(2,128)} %bitcast.18, bf16[64,1792]{1,0:T(8,128)(2,1)} %bitcast.14, bf16[64,128]{1,0:T(8,128)(2,1)} %bitcast.17, bf16[64,1792]{1,0:T(8,128)(2,1)} %bitcast.15, bf16[1,512]{1,0:T(2,128)(2,1)} %gain_ref.1, ...), custom_call_target="tpu_custom_call" | custom-call | tf_op jit(solution)/shard_map/pallas_call | solution.py:580
  133.1 0.0 copy-start.1
  133.1 1.6 %copy.13 = bf16[1,2,1,64,512]{4,3,2,1,0:T(8,128)(2,1)} copy(bf16[1,2,1,64,512]{4,3,2,1,0:T(8,128)(2,1)} %bitcast.16) | data formatting | bytes 262144
  134.7 0.0 copy-done.1
  134.7 0.6 copy.14
Async XLA Ops:
  0.6 0.7 copy-start
  133.1 1.6 %copy-start.1 = (f32[2,64]{1,0:T(2,128)S(1)}, f32[2,64]{1,0:T(2,128)}, u32[]{:S(2)}) copy-start(f32[2,64]{1,0:T(2,128)} %get-tuple-element.5) | copy-start | bytes 1540

commit v5 on v4

--- a/solution.py
+++ b/solution.py
@@ -215,7 +215,7 @@
 
     cut_send(l, jnp.broadcast_to(seen, (rows, width)))
 
-    early = min(3, up_steps)
+    early = min(2, up_steps)
     for s in range(early):
         ring_step(s)
         if s == 0:

time: 135 us -> 140 us (1.037)
  Pallas kernels: 131 us -> 136 us
    pallas_call x1, Pallas kernels: 131 us -> 136 us  [body(): pl.pallas_call(functools.partial(kernel, n, nd), out_shape=(jax.ShapeDtyp...]
where the time goes in v5:
time: 140 us
  Pallas kernels  136 us (97%)
  local copies, waits for them, and re-layouts  3.41 us (2%)
    pallas_call x1, Pallas kernels, body(): pl.pallas_call(functools.partial(kernel, n, nd), out_shape=(jax.ShapeDtyp...  136 us
    unnamed x6, local copies, waits for them, and re-layouts  2.81 us

profile of v5, /device:TPU:1, one launch (start us, length us, event | category | flops | bytes accessed | tf_op | source)
XLA Modules:
  0.0 140.0 jit_solution(15258219667065518465)
XLA Ops:
  0.6 0.0 copy-start
  0.6 0.7 copy-done
  1.3 0.6 reshape.21.read_ref
  1.9 136.0 %shard_map.86 = (bf16[2,64,512]{2,1,0:T(8,128)(2,1)}, f32[2,64]{1,0:T(2,128)}) custom-call(bf16[128,1792]{1,0:T(8,128)(2,1)} %bitcast.13, s32[2,4]{1,0:T(2,128)} %bitcast.18, bf16[64,1792]{1,0:T(8,128)(2,1)} %bitcast.14, bf16[64,128]{1,0:T(8,128)(2,1)} %bitcast.17, bf16[64,1792]{1,0:T(8,128)(2,1)} %bitcast.15, bf16[1,512]{1,0:T(2,128)(2,1)} %gain_ref.1, ...), custom_call_target="tpu_custom_call" | custom-call | tf_op jit(solution)/shard_map/pallas_call | solution.py:580
  137.9 0.0 copy-start.1
  137.9 1.6 %copy.13 = bf16[1,2,1,64,512]{4,3,2,1,0:T(8,128)(2,1)} copy(bf16[1,2,1,64,512]{4,3,2,1,0:T(8,128)(2,1)} %bitcast.16) | data formatting | bytes 262144
  139.5 0.0 copy-done.1
  139.5 0.6 copy.14
Async XLA Ops:
  0.6 0.7 copy-start
  137.9 1.6 %copy-start.1 = (f32[2,64]{1,0:T(2,128)S(1)}, f32[2,64]{1,0:T(2,128)}, u32[]{:S(2)}) copy-start(f32[2,64]{1,0:T(2,128)} %get-tuple-element.5) | copy-start | bytes 1540
